TPU v7x, 128 devices: a whole 4x4x4 slice. The times are simulated.
128 devices in a mesh: src: 8 (over x, core), tgt: 16 (over y, z).
Axes of the slice: x: 4, y: 4, z: 4, core: 2. Of those that a mesh axis runs over, the one named last changes fastest.
Arguments:
- source_points: float32 [3, 524288], P(None, ('src', 'tgt')), may hold values from 0 to 2
- source_values: bfloat16 [524288, 128], P(('src', 'tgt')), may hold values from -0.031982422 to 0.033935547
- leaf_index: int32 [1024, 512], P(('src', 'tgt')), may hold values from 0 to 4095, as said below
- leaf_pivots: int32 [1024, 256], P(('src', 'tgt')), may hold values from 0 to 511, as said below
- leaf_proj: bfloat16 [1024, 256, 512], P(('src', 'tgt')), may hold values from -0.25 to 0.25
- node_pivots: int32 [128, 256], P(('src', 'tgt')), may hold values from 0 to 2047, as said below
- node_proj: bfloat16 [128, 256, 2048], P(('src', 'tgt')), may hold values from -0.125 to 0.125
- top_pivots: int32 [16, 256], P('tgt'), may hold values from 0 to 2047, as said below
- top_proj: bfloat16 [16, 256, 2048], P('tgt', None, 'src'), may hold values from -0.125 to 0.125
- target_points: float32 [3, 65536], P(None, 'tgt'), may hold values from 0 to 2
- near_list: int32 [8, 256, 8], P('src', 'tgt'), may hold values from 0 to 23, as said below
- near_count: int32 [8, 256], P('src', 'tgt'), may hold values from 0 to 8, as said below
- far_list: int32 [8, 256, 12], P('src', 'tgt'), may hold values from 0 to 23, as said below
- far_count: int32 [8, 256], P('src', 'tgt'), may hold values from 0 to 12, as said below
- node_list: int32 [8, 256, 4], P('src', 'tgt'), may hold values from 0 to 15, as said below
- node_count: int32 [8, 256], P('src', 'tgt'), may hold values from 0 to 4, as said below
- top_list: int32 [256, 12], P('tgt'), may hold values from 0 to 15, as said below
- top_count: int32 [256], P('tgt'), may hold values from 1 to 12, as said below
Outputs:
- posterior: float32 [65536, 128], P('tgt', 'src')
Inputs may be any that keep to these rules, and one draw needn't show every extreme that they name: `leaf_index`: each block of 8 rows (one node) holds every number of 0 to 4095 once. `leaf_pivots`: entries of a row are distinct. `node_pivots`: entries of a row are distinct. `top_pivots`: entries of a row are distinct. `near_list`: entries of a row are distinct and differ from those of far_list in the same row. `far_list`: entries of a row are distinct. `near_count`: zero for target leaves whose block differs from i by more than one; in each block and column some target leaf reaches 8. `far_count`: zero for target leaves whose block differs from i by more than one; in each block and column some target leaf reaches 12. `node_list`: entries of a row are distinct. `node_count`: zero for target leaves whose block differs from i by at most one; in each block and column some target leaf reaches 4. `top_list`: entries of a row are distinct. `top_count`: in each column some target leaf reaches 12.
All inputs are finite; a program needn't handle non-finite values.
Results may differ from a plain program's by a relative error of at most 0.0075.
Values may be sent and summed in bfloat16 or wider, within the bound.
No kernel may reach another device: no remote copies, remote signals or barrier semaphores. Data moves between devices by JAX's collectives and lax.ppermute only.
A program may use at most 64 MiB of HBM per device.

v0:
```python
import functools

import jax
import jax.numpy as jnp
from jax import lax
from jax.experimental import pallas as pl
from jax.experimental.pallas import tpu as pltpu
from jax.sharding import PartitionSpec as P

SL = 8
LEAF = 512
SKEL = 256
Q = 128
TLEAF = 256
TL_J = 16
WIN = 6
KF = 16
LN2 = 0.6931471805599453
SCALE = 2.0 / LN2
GROUP = 16
TAIL = 4
VMEM = pltpu.VMEM
SMEM = pltpu.SMEM
bf16 = jnp.bfloat16
f32 = jnp.float32
NEAR_AT, FAR_AT, NODE_AT = 0, 8, 20
NEAR_N, FAR_N, NODE_N = 24, 25, 26
LIST_ROWS = 32
POINT_ROWS = 96
TRASH = 16
PART = 384
BIG = 60
OUT = pltpu.VMEM
HALO_COST = 6e9
OWN_COST = 5e9
NODE_COST = 6e9
TOP_COST = 6e9


def split2(x):
    high = x.astype(bf16).astype(f32)
    return high, (x - high).astype(bf16).astype(f32)


def split3(x):
    high, rest = split2(x)
    return high, rest, (x - high - rest).astype(bf16).astype(f32)


def centred(x):
    return (x - 1.0) * SCALE


def features(coords, is_source):
    pieces = [split2(c) for c in coords]
    high = [p[0] for p in pieces]
    low = [p[1] for p in pieces]
    norm = sum((h + r) * (h + r) for h, r in pieces)
    norms = list(split3(norm))
    one = jnp.ones_like(norm)
    zero = jnp.zeros_like(norm)
    if is_source:
        high = [-2.0 * h for h in high]
        low = [-2.0 * r for r in low]
        return high + low + high + [one, one, one] + norms + [zero]
    return high + high + low + norms + [one, one, one] + [zero]


def matern(w):
    w = jnp.maximum(w, 1e-12)
    u = w * lax.rsqrt(w)
    return ((1.0 + LN2 * u) * jnp.exp2(-u)).astype(bf16)


def take(row, index):
    return jnp.take_along_axis(row, index, axis=1, mode="promise_in_bounds")


def pick(chunks, index):
    low = index & 127
    high = index >> 7
    result = jnp.zeros((8, 128), f32)
    for k, chunk in enumerate(chunks):
        result = jnp.where(high == k, take(chunk, low), result)
    return result


def lanes(x, m):
    return x[:, 128 * m : 128 * (m + 1)]


def place():
    src = lax.axis_index("src")
    tgt = lax.axis_index("tgt")
    start = jnp.clip(2 * src - 2, 0, TL_J - WIN)
    return src, src >> 1, src & 1, tgt >> 2, tgt & 3, start


def leaf_kernel(
    idx_h, piv_h, npiv_h, tpiv_h, pts_h, vals_h, proj_h, nproj_h, tproj_h,
    tpts_h, near_h, far_h, node_h, nearn_h, farn_h, noden_h,
    v_out, f_out, n_out, t_out, held_out, lists_out, idx, piv, npiv, tpiv, pts, vals, proj, nproj, tproj,
    tpts, near, far, node, nearn, farn, noden, wide, gathered, fs, ns, idx_s, sems,
):
    src, chip, _, _, _, _ = place()
    rows = vals.shape[0]
    moves = [(pts_h, pts), (idx_h, idx), (piv_h, piv), (npiv_h, npiv), (tpiv_h, tpiv), (vals_h, vals),
             (proj_h, proj), (nproj_h, nproj), (tproj_h, tproj), (tpts_h, tpts), (near_h, near), (far_h, far),
             (node_h, node), (nearn_h, nearn), (farn_h, farn), (noden_h, noden)]
    copies = [pltpu.make_async_copy(a, b, sems.at[k]) for k, (a, b) in enumerate(moves)]
    for leaf in range(SL):
        copies.append(pltpu.make_async_copy(idx_h.at[leaf], idx_s.at[pl.ds(LEAF * leaf, LEAF)], sems.at[16 + leaf]))
    for copy in copies:
        copy.start()
    for copy in copies[:5]:
        copy.wait()
    index = idx[...]
    pivots = piv[...]
    node_piv = jnp.broadcast_to(npiv[...], (8, SKEL))
    top_piv = jnp.broadcast_to(tpiv[...], (8, SKEL))
    leaf_of = lax.broadcasted_iota(jnp.int32, (8, 128), 0)
    leaf_c, skel_c, node_c, top_c = [], [], [], []
    for c in range(3):
        chunks = [jnp.broadcast_to(pts[c : c + 1, 128 * k : 128 * (k + 1)], (8, 128)) for k in range(rows // 128)]
        leaf_x = [pick(chunks, lanes(index, m)) for m in range(4)]
        skel_x = [pick(leaf_x, lanes(pivots, m)) for m in range(2)]
        node_x = []
        top_x = []
        for m in range(2):
            at = lanes(node_piv, m)
            mine = jnp.where(leaf_of == (at >> 8), pick(skel_x, at & 255), 0.0)
            node_x.append(jnp.broadcast_to(jnp.sum(mine, axis=0, keepdims=True), (8, 128)))
        for m in range(2):
            at = lanes(top_piv, m)
            top_x.append(jnp.where((at >> 8) == src, centred(pick(node_x, at & 255)), 0.0))
        leaf_c.append(centred(jnp.concatenate(leaf_x, axis=1)))
        skel_c.append(centred(jnp.concatenate(skel_x, axis=1)))
        node_c.append(centred(jnp.concatenate(node_x, axis=1)))
        top_c.append(jnp.concatenate(top_x, axis=1))
    for f, (a, b, n) in enumerate(zip(features(leaf_c, True), features(skel_c, True), features(node_c, True))):
        for leaf in range(SL):
            fs[2 * leaf, f : f + 1, :] = a[leaf : leaf + 1, :256]
            fs[2 * leaf + 1, f : f + 1, :] = a[leaf : leaf + 1, 256:]
            fs[16 + leaf, f : f + 1, :] = b[leaf : leaf + 1, :]
        ns[f : f + 1, :] = n[0:1, :]
    f_out[...] = fs[...].astype(bf16)
    n_out[256:272, :] = ns[:, :128].astype(bf16)
    n_out[272:288, :] = ns[:, 128:].astype(bf16)
    ns[...] = jnp.zeros_like(ns)
    for c in range(3):
        for k, piece in enumerate(split3(top_c[c])):
            ns[3 * c + k : 3 * c + k + 1, :] = piece[0:1, :]
    pieces = ns[...].astype(bf16)
    for copy in copies[9:]:
        copy.wait()
    step = POINT_ROWS // 3
    for c in range(3):
        for k in range(step):
            held_out[step * c + k : step * c + k + 1, :] = tpts[c : c + 1, 128 * k : 128 * k + 128]
    lists_out[...] = jnp.zeros_like(lists_out)
    lists_out[NEAR_AT : FAR_AT, :] = near[0]
    for e in range(NODE_AT - FAR_AT):
        lists_out[FAR_AT + e : FAR_AT + e + 1, :] = far[e]
    lists_out[NODE_AT : NEAR_N, :] = node[0]
    lists_out[NEAR_N : NEAR_N + 1, :] = nearn[...]
    lists_out[FAR_N : FAR_N + 1, :] = farn[...]
    lists_out[NODE_N : NODE_N + 1, :] = noden[...]
    held_out[POINT_ROWS:, :] = jnp.zeros((LIST_ROWS, 128), f32)
    held_out[POINT_ROWS:, :TL_J] = lists_out[...].astype(f32)
    copies[5].wait()

    def widen(k, _):
        at = pl.multiple_of(k * 512, 512)
        wide[pl.ds(at, 512), :] = vals[pl.ds(at, 512), :].astype(f32)
        return 0

    lax.fori_loop(0, rows // 512, widen, 0)

    def gather(k, _):
        at = pl.multiple_of(k * 64, 64)
        for r in range(64):
            gathered[pl.ds(at + r, 1), :] = wide[pl.ds(idx_s[at + r], 1), :]
        return 0

    lax.fori_loop(0, rows // 64, gather, 0)
    for copy in copies[6:9]:
        copy.wait()

    for leaf in range(SL):
        leaf_vals = gathered[leaf * LEAF : (leaf + 1) * LEAF, :].astype(bf16)
        v_out[2 * leaf] = leaf_vals[:256]
        v_out[2 * leaf + 1] = leaf_vals[256:]
        v_out[16 + leaf] = jnp.dot(proj[leaf], leaf_vals, preferred_element_type=f32).astype(bf16)
    node_vals = jnp.dot(
        nproj[0], v_out[16:24].reshape(SL * SKEL, Q), preferred_element_type=f32
    ).astype(bf16)
    n_out[0:256, :] = node_vals
    top = jnp.dot(tproj[0], node_vals, preferred_element_type=f32).T

    for half in range(2):
        for x in range(4):
            part = top[32 * x : 32 * x + 32, 128 * half : 128 * half + 128]
            at = (x - chip) & 3
            t_out[at, 48 * half : 48 * half + 32, :] = part.astype(bf16)
            t_out[at, 48 * half + 32 : 48 * half + 48, :] = lanes(pieces, half)


def target_rows(held, first, count, fa):
    step = TL_J * TLEAF // 128
    rows = features([centred(held[pl.ds(step * c + first, count), :]) for c in range(3)], False)
    for f, row in enumerate(rows):
        for k in range(count):
            fa[f : f + 1, 128 * k : 128 * k + 128] = row[k : k + 1, :]


def set_targets(fa, a_ref, count):
    for t in range(count):
        a_ref[t] = fa[:, TLEAF * t : TLEAF * t + TLEAF].T.astype(bf16)
    a_ref[count] = jnp.zeros((TLEAF, KF), bf16)


def run_pairs(pairs, n, trash, a_ref, f_ref, v_of, acc):
    for r in range(TAIL - 1):
        pairs[n + r] = trash

    def group(first, size):
        for q in range(size):
            pair = pairs[first + q]
            s = pair >> 5
            t = pair & 31
            w = jnp.dot(a_ref[t], f_ref[s], preferred_element_type=f32)
            acc[t] += jnp.dot(matern(w), v_of(s), preferred_element_type=f32)

    def large(g, _):
        group(g * GROUP, GROUP)
        return 0

    def small(g, _):
        group(done + g * TAIL, TAIL)
        return 0

    turns = n // GROUP
    done = turns * GROUP
    lax.fori_loop(0, turns, large, 0)
    lax.fori_loop(0, (n - done + TAIL - 1) // TAIL, small, 0)


def leaf_pairs(pairs, lists, start, base):
    def target(t, n):
        leaf = start + t
        near, far = lists[NEAR_N, leaf], lists[FAR_N, leaf]
        for e in range(FAR_AT):
            v = lists[NEAR_AT + e, leaf] - base
            pairs[n] = 64 * v + t
            pairs[n + 1] = 64 * v + 32 + t
            n = n + jnp.where((v >= 0) & (v < SL) & (e < near), 2, 0)
        for e in range(NODE_AT - FAR_AT):
            v = lists[FAR_AT + e, leaf] - base
            pairs[n] = 512 + 32 * v + t
            n = n + jnp.where((v >= 0) & (v < SL) & (e < far), 1, 0)
        return n

    return lax.fori_loop(0, WIN, target, 0)


def clear(acc):
    def one(t, _):
        acc[t] = jnp.zeros(acc.shape[1:], f32)
        return 0

    lax.fori_loop(0, acc.shape[0], one, 0)


def halo_kernel(base, lists, held, v_ref, f_ref, after, out, fa, a_ref, acc, pairs):
    start = place()[5]
    clear(acc)
    target_rows(held, 2 * start, 2 * WIN, fa)
    set_targets(fa, a_ref, WIN)
    n = leaf_pairs(pairs, lists, start, base)
    run_pairs(pairs, n, WIN, a_ref, f_ref, lambda s: v_ref[s], acc)
    for t in range(WIN):
        out[t * TLEAF : (t + 1) * TLEAF, :] = acc[t].astype(bf16)


def own_kernel(lists, held, v_ref, f_ref, after, out, a_all, fa, a_ref, pairs):
    start = place()[5]
    clear(out)
    target_rows(held, 0, 2 * TL_J, fa)
    set_targets(fa, a_all, TL_J)
    for t in range(WIN):
        a_ref[t] = a_all[start + t]
    a_ref[WIN] = jnp.zeros((TLEAF, KF), bf16)
    n = leaf_pairs(pairs, lists, start, SL)
    run_pairs(pairs, n, WIN, a_ref, f_ref, lambda s: v_ref[s], out)


def slot_of(column, row, plane):
    return 4 * ((row - (column >> 2)) & 3) + ((plane - (column & 3)) & 3)


def node_kernel(
    lists, own, a_ref, halo_l, halo_r, top, y0, y1, y2, y3,
    out, acc, ys, f_ref, pairs, sems,
):
    _, chip, core, row, plane, start = place()
    copies = [pltpu.make_async_copy(y, ys.at[k], sems.at[k]) for k, y in enumerate((y0, y1, y2, y3))]
    for copy in copies:
        copy.start()
    clear(acc)
    for t in range(WIN):
        sides = halo_l[t * TLEAF : (t + 1) * TLEAF, :].astype(f32) + halo_r[t * TLEAF : (t + 1) * TLEAF, :].astype(f32)
        acc[start + t] = own[t] + sides

    def target(t, n):
        for e in range(NEAR_N - NODE_AT):
            pairs[n + e] = 32 * slot_of(lists[NODE_AT + e, t], row, plane) + t
        return n + lists[NODE_N, t]

    n = lax.fori_loop(0, TL_J, target, 0)
    for copy in copies:
        copy.wait()
    for k in range(4):
        for z in range(4):
            f_ref[4 * k + z, :, 0:128] = ys[k, z * PART + 256 : z * PART + 272, :]
            f_ref[4 * k + z, :, 128:256] = ys[k, z * PART + 272 : z * PART + 288, :]

    def node_vals(s):
        return ys[s >> 2, pl.ds(pl.multiple_of((s & 3) * PART, 32), SKEL), :]

    run_pairs(pairs, n, TRASH, a_ref, f_ref, node_vals, acc)

    def turn(t, _):
        at = pl.multiple_of(t * TLEAF, TLEAF)
        block = acc[t].T
        for x in range(4):
            for k in range(2):
                begin = 16 * (2 * x + k)
                out[k ^ core, (x - chip) & 3, :, pl.ds(at, TLEAF)] = block[begin : begin + 16]
        return 0

    lax.fori_loop(0, TL_J, turn, 0)
    for t in range(TL_J // 2):
        at = pl.multiple_of((core * (TL_J // 2) + t) * TLEAF, TLEAF)
        for k in range(2):
            out[k, 0, :, pl.ds(at, TLEAF)] += top[k, :, t * TLEAF : (t + 1) * TLEAF]


def top_pairs(pairs, listed, counts, row, plane, first, count):
    def target(t, n):
        for e in range(listed.shape[1]):
            pairs[n + e] = 32 * slot_of(listed[first + t, e], row, plane) + t
        return n + counts[first + t]

    return lax.fori_loop(0, count, target, 0)


def top_kernel(listed, counts, a_all, y0, y1, y2, y3, out, f_ref, v_ref, a_ref, acc, pw, fw, pairs):
    count = TL_J // 2
    _, _, core, row, plane, _ = place()
    first = core * count
    for dy, ys in enumerate((y0, y1, y2, y3)):
        for dz in range(4):
            slot = 4 * dy + dz
            for half in range(2):
                at = dz * PART + 288 + 48 * half
                vals = ys[at : at + 32, :].astype(f32)
                v_ref[slot, 128 * half : 128 * half + 128, :] = vals.T.astype(bf16)
                pieces = ys[at + 32 : at + 48, :].astype(f32)
                line = 2 * slot + half
                for p in range(9):
                    pw[p, line : line + 1, :] = pieces[p : p + 1]
    coords = [pw[3 * c] + pw[3 * c + 1] + pw[3 * c + 2] for c in range(3)]
    for f, lines in enumerate(features(coords, True)):
        for line in range(32):
            half = line % 2
            fw[line // 2, f : f + 1, 128 * half : 128 * half + 128] = lines[line : line + 1, :]
    f_ref[...] = fw[...].astype(bf16)
    for t in range(count):
        a_ref[t] = a_all[first + t]
    a_ref[count] = jnp.zeros((TLEAF, KF), bf16)
    clear(acc)
    n = top_pairs(pairs, listed, counts, row, plane, first, count)
    run_pairs(pairs, n, count, a_ref, f_ref, lambda s: v_ref[s], acc)
    for t in range(count):
        block = acc[t].T
        for k in range(2):
            out[k ^ core, :, t * TLEAF : (t + 1) * TLEAF] = block[16 * k : 16 * k + 16]


def whole(count):
    return [pl.BlockSpec(memory_space=VMEM)] * count


def params(mebibytes):
    return pltpu.CompilerParams(vmem_limit_bytes=mebibytes << 20)


def cost(flops, moved):
    return pl.CostEstimate(flops=int(flops), bytes_accessed=int(moved), transcendentals=0)


def pair_scratch():
    return [pltpu.SMEM((512,), jnp.int32)]


def shift(axis, count, fn):
    return [(i, fn(i)) for i in range(count) if 0 <= fn(i) < count]


def shards(
    source_points, source_values, leaf_index, leaf_pivots, leaf_proj, node_pivots, node_proj,
    top_pivots, top_proj, target_points, near_list, near_count, far_list, far_count,
    node_list, node_count, top_list, top_count,
):
    smem = pl.BlockSpec(memory_space=SMEM)
    anywhere = pl.BlockSpec(memory_space=pl.ANY)
    v_all, f_all, node_own, top_own, held, lists = pl.pallas_call(
        leaf_kernel,
        out_shape=(
            OUT((24, 256, Q), bf16),
            OUT((24, KF, 256), bf16),
            OUT((288, Q), bf16),
            OUT((4, 96, 128), bf16),
            OUT((POINT_ROWS + LIST_ROWS, 128), f32),
            OUT((LIST_ROWS, TL_J), jnp.int32),
        ),
        in_specs=[anywhere] * 16,
        out_specs=tuple(whole(6)),
        scratch_shapes=[
            VMEM((8, 512), jnp.int32),
            VMEM((8, 256), jnp.int32),
            VMEM((1, 256), jnp.int32),
            VMEM((1, 256), jnp.int32),
            VMEM((3, 4096), f32),
            VMEM((4096, Q), bf16),
            VMEM((8, 256, 512), bf16),
            VMEM((1, 256, 2048), bf16),
            VMEM((1, 256, 256), bf16),
            VMEM((3, 4096), f32),
            VMEM((1, 8, TL_J), jnp.int32),
            VMEM((12, 1, TL_J), jnp.int32),
            VMEM((1, 4, TL_J), jnp.int32),
            VMEM((1, TL_J), jnp.int32),
            VMEM((1, TL_J), jnp.int32),
            VMEM((1, TL_J), jnp.int32),
            VMEM((4096, Q), f32),
            VMEM((4096, Q), f32),
            VMEM((24, KF, 256), f32),
            VMEM((KF, 256), f32),
            pltpu.SMEM((4096,), jnp.int32),
            pltpu.SemaphoreType.DMA((24,)),
        ],
        compiler_params=params(BIG),
        cost_estimate=cost(8e9, 8e6),
        name="leaf_stage",
    )(leaf_index, leaf_pivots, node_pivots, top_pivots, source_points, source_values,
      leaf_proj, node_proj, top_proj, target_points, near_list.transpose(0, 2, 1), far_list.transpose(2, 0, 1),
      node_list.transpose(0, 2, 1), near_count, far_count, node_count)
    forward = shift("tgt", 16, lambda i: i + 1)
    backward = shift("tgt", 16, lambda i: i - 1)
    held_l = lax.ppermute(held, "tgt", forward)
    held_r = lax.ppermute(held, "tgt", backward)
    lists_l = held_l[POINT_ROWS:, :TL_J].astype(jnp.int32)
    lists_r = held_r[POINT_ROWS:, :TL_J].astype(jnp.int32)

    zshift = [shift("tgt", 16, lambda i, d=d: (i // 4) * 4 + (i % 4 + d) % 4) for d in range(4)]
    yshift = [shift("tgt", 16, lambda i, d=d: ((i // 4 + d) % 4) * 4 + i % 4) for d in range(4)]
    xshift = [shift("src", 8, lambda i, d=d: (i + 2 * d) % 8) for d in range(4)]
    cores = shift("src", 8, lambda i: i ^ 1)

    def others(x, axis, shifts):
        return [lax.ppermute(x, axis, shifts[d]) for d in (1, 3, 2)]

    def in_order(x, got):
        return [x, got[0], got[2], got[1]]

    top_pair = top_own.astype(f32) + lax.ppermute(top_own, "src", cores).astype(f32)
    top_sum = top_pair[0]
    for d in (1, 3, 2):
        top_sum = top_sum + lax.ppermute(top_pair[d].astype(bf16), "src", xshift[d]).astype(f32)
    parts = jnp.concatenate([node_own, top_sum.astype(bf16)], axis=0)
    bundle = jnp.concatenate(in_order(parts, others(parts, "tgt", zshift)), axis=0)
    ys = in_order(bundle, others(bundle, "tgt", yshift))

    def halo(base, lists_of, held_of, after):
        return pl.pallas_call(
            functools.partial(halo_kernel, base),
            out_shape=jax.ShapeDtypeStruct((WIN * TLEAF, Q), bf16),
            in_specs=[smem] + whole(3) + [anywhere],
            out_specs=pl.BlockSpec(memory_space=VMEM),
            scratch_shapes=[
                VMEM((KF, WIN * TLEAF), f32),
                VMEM((WIN + 1, TLEAF, KF), bf16),
                VMEM((WIN + 1, TLEAF, Q), f32),
            ] + pair_scratch(),
            compiler_params=params(24),
            cost_estimate=cost(HALO_COST, 3e6),
            name="halo_terms",
        )(lists_of, held_of, v_all, f_all, after)

    to_l = halo(16, lists_l, held_l, parts)
    got_r = lax.ppermute(to_l, "tgt", backward)
    to_r = halo(0, lists_r, held_r, bundle)
    got_l = lax.ppermute(to_r, "tgt", forward)

    own, a_all = pl.pallas_call(
        own_kernel,
        out_shape=(
            jax.ShapeDtypeStruct((WIN + 1, TLEAF, Q), f32),
            jax.ShapeDtypeStruct((TL_J + 1, TLEAF, KF), bf16),
        ),
        in_specs=[smem] + whole(3) + [anywhere],
        out_specs=tuple(whole(2)),
        scratch_shapes=[
            VMEM((KF, TL_J * TLEAF), f32),
            VMEM((WIN + 1, TLEAF, KF), bf16),
        ] + pair_scratch(),
        compiler_params=params(24),
        cost_estimate=cost(OWN_COST, 3e6),
        name="own_terms",
    )(lists, held, v_all, f_all, to_r)

    half = TL_J // 2
    top_term = pl.pallas_call(
        top_kernel,
        out_shape=jax.ShapeDtypeStruct((2, 16, half * TLEAF), f32),
        in_specs=[smem, smem] + whole(5),
        out_specs=pl.BlockSpec(memory_space=VMEM),
        scratch_shapes=[
            VMEM((16, KF, 256), bf16),
            VMEM((16, 256, 32), bf16),
            VMEM((half + 1, TLEAF, KF), bf16),
            VMEM((half + 1, TLEAF, 32), f32),
            VMEM((9, 32, 128), f32),
            VMEM((16, KF, 256), f32),
        ] + pair_scratch(),
        compiler_params=params(24),
        cost_estimate=cost(TOP_COST, 3e6),
        name="top_terms",
    )(top_list, top_count, a_all, *ys)

    partial = pl.pallas_call(
        node_kernel,
        out_shape=jax.ShapeDtypeStruct((2, 4, 16, TL_J * TLEAF), f32),
        in_specs=[smem] + whole(5) + [anywhere] * 4,
        out_specs=pl.BlockSpec(memory_space=VMEM),
        scratch_shapes=[
            VMEM((TL_J + 1, TLEAF, Q), f32),
            VMEM((4, 4 * PART, Q), bf16),
            VMEM((16, KF, 256), bf16),
        ] + pair_scratch() + [pltpu.SemaphoreType.DMA((4,))],
        compiler_params=params(24),
        cost_estimate=cost(NODE_COST, 3e6),
        name="node_terms",
    )(lists, own, a_all, got_l, got_r, top_term, *ys)

    pair = partial[0] + lax.ppermute(partial[1], "src", cores)
    total = pair[0]
    for d in (1, 3, 2):
        total = total + lax.ppermute(pair[d].astype(bf16), "src", xshift[d]).astype(f32)
    return total.T


def solution(mesh):
    both = ("src", "tgt")
    in_specs = (
        P(None, both), P(both, None), P(both, None), P(both, None), P(both, None, None), P(both, None),
        P(both, None, None), P("tgt", None), P("tgt", None, "src"), P(None, "tgt"), P("src", "tgt", None),
        P("src", "tgt"), P("src", "tgt", None), P("src", "tgt"), P("src", "tgt", None), P("src", "tgt"),
        P("tgt", None), P("tgt"),
    )
    return jax.shard_map(shards, mesh=mesh, in_specs=in_specs, out_specs=P("tgt", "src"), check_vma=False)
```

profile of v0, /device:TPU:8, one launch (start us, length us, event | category | flops | bytes accessed | tf_op | source)
XLA Modules:
  0.0 97.3 jit_solution(11819961420938412110)
XLA Ops:
  0.0 7.5 %leaf_stage.1 = (bf16[24,256,128]{2,1,0:T(8,128)(2,1)S(1)}, bf16[24,16,256]{2,1,0:T(8,128)(2,1)S(1)}, bf16[288,128]{1,0:T(8,128)(2,1)S(1)}, bf16[4,96,128]{2,1,0...) custom-call(s32[8,512]{1,0:T(8,128)} %idx_h.1, s32[8,256]{1,0:T(8,128)} %piv_h.1, s32[1,256]{1,0:T(1,128)} %npiv_h.1, ...), custom_call_target="tpu_custom_call" | custom-call | flops 8000000000 | bytes 8000000 | tf_op jit(solution)/shard_map/leaf_stage/pallas_call | solution.py:417
  7.5 3.8 %collective-permute-start.9 = (f32[128,128]{1,0:T(8,128)S(1)}, f32[128,128]{1,0:T(8,128)S(1)}, u32[]{:S(2)}, u32[]{:S(2)}) collective-permute-start(f32[128,128]{1,0:T(8,128)S(1)} %get-tuple-element.14.held), channel_id=1, source_target_pairs={{0,1},{1,2},{2,3},{3,4},{4,5},{5,6},{6,7},{7,8},{8,9},{9,10},{10,1... | collective-permute-start | bytes 196616 | tf_op jit(solution)/shard_map/ppermute | solution.py:461
  11.4 4.1 %collective-permute-start = (f32[128,128]{1,0:T(8,128)S(1)}, f32[128,128]{1,0:T(8,128)S(1)}, u32[]{:S(2)}, u32[]{:S(2)}) collective-permute-start(f32[128,128]{1,0:T(8,128)S(1)} %get-tuple-element.14.held), channel_id=1, source_target_pairs={{1,0},{2,1},{3,2},{4,3},{5,4},{6,5},{7,6},{8,7},{9,8},{10,9},{11,1... | collective-permute-start | bytes 196616 | tf_op jit(solution)/shard_map/ppermute | solution.py:462
  15.5 0.1 collective-permute-start.1
  15.6 0.2 collective-permute-done.9.held
  15.8 1.1 %collective-permute-done.1 = bf16[4,96,128]{2,1,0:T(8,128)(2,1)S(1)} collective-permute-done((bf16[4,96,128]{2,1,0:T(8,128)(2,1)S(1)}, bf16[4,96,128]{2,1,0:T(8,128)(2,1)S(1)}, u32[]{:S(2)}, u32[]{:S(2)}) %collective-permute-start.1) | collective-permute-done | bytes 98336 | tf_op jit(solution)/shard_map/ppermute | solution.py:477
  16.9 1.6 %collective-permute-start.2 = (bf16[96,128]{1,0:T(8,128)(2,1)S(1)}, bf16[96,128]{1,0:T(8,128)(2,1)S(1)}, u32[]{:S(2)}, u32[]{:S(2)}) collective-permute-start(bf16[96,128]{1,0:T(8,128)(2,1)S(1)} %get-tuple-element.30), channel_id=1, source_target_pairs={{0,32},{16,48},{32,64},{48,80},{64,96},{80,112},{96,0},{112,16},{1... | collective-permute-start | bytes 73736 | tf_op jit(solution)/shard_map/ppermute | solution.py:480
  18.5 2.7 %collective-permute-start.4 = (bf16[96,128]{1,0:T(8,128)(2,1)S(1)}, bf16[96,128]{1,0:T(8,128)(2,1)S(1)}, u32[]{:S(2)}, u32[]{:S(2)}) collective-permute-start(bf16[96,128]{1,0:T(8,128)(2,1)S(1)} %get-tuple-element.31), channel_id=1, source_target_pairs={{0,64},{16,80},{32,96},{48,112},{64,0},{80,16},{96,32},{112,48},{1... | collective-permute-start | bytes 73736 | tf_op jit(solution)/shard_map/ppermute | solution.py:480
  21.2 1.5 %collective-permute-start.3 = (bf16[96,128]{1,0:T(8,128)(2,1)S(1)}, bf16[96,128]{1,0:T(8,128)(2,1)S(1)}, u32[]{:S(2)}, u32[]{:S(2)}) collective-permute-start(bf16[96,128]{1,0:T(8,128)(2,1)S(1)} %get-tuple-element.32), channel_id=1, source_target_pairs={{0,96},{16,112},{32,0},{48,16},{64,32},{80,48},{96,64},{112,80},{1... | collective-permute-start | bytes 73736 | tf_op jit(solution)/shard_map/ppermute | solution.py:480
  22.7 0.0 collective-permute-done.held
  22.7 0.0 collective-permute-done.2
  22.7 1.1 %collective-permute-done.4 = bf16[96,128]{1,0:T(8,128)(2,1)S(1)} collective-permute-done((bf16[96,128]{1,0:T(8,128)(2,1)S(1)}, bf16[96,128]{1,0:T(8,128)(2,1)S(1)}, u32[]{:S(2)}, u32[]{:S(2)}) %collective-permute-start.4) | collective-permute-done | bytes 24608 | tf_op jit(solution)/shard_map/ppermute | solution.py:480
  23.8 1.2 %collective-permute-done.3 = bf16[96,128]{1,0:T(8,128)(2,1)S(1)} collective-permute-done((bf16[96,128]{1,0:T(8,128)(2,1)S(1)}, bf16[96,128]{1,0:T(8,128)(2,1)S(1)}, u32[]{:S(2)}, u32[]{:S(2)}) %collective-permute-start.3) | collective-permute-done | bytes 24608 | tf_op jit(solution)/shard_map/ppermute | solution.py:480
  25.1 2.0 %collective-permute-start.7 = (bf16[384,128]{1,0:T(8,128)(2,1)S(1)}, bf16[384,128]{1,0:T(8,128)(2,1)S(1)}, u32[]{:S(2)}, u32[]{:S(2)}) collective-permute-start(bf16[384,128]{1,0:T(8,128)(2,1)S(1)} %pad_maximum_fusion.after), channel_id=1, source_target_pairs={{0,3},{1,0},{2,1},{3,2},{4,7},{5,4},{6,5},{7,6},{8,11},{9,8},{10,9... | collective-permute-start | bytes 294920 | tf_op jit(solution)/shard_map/ppermute | solution.py:472
  27.1 0.0 collective-permute-start.6
  27.1 1.3 %collective-permute-start.5 = (bf16[384,128]{1,0:T(8,128)(2,1)S(1)}, bf16[384,128]{1,0:T(8,128)(2,1)S(1)}, u32[]{:S(2)}, u32[]{:S(2)}) collective-permute-start(bf16[384,128]{1,0:T(8,128)(2,1)S(1)} %pad_maximum_fusion.after), channel_id=1, source_target_pairs={{0,1},{1,2},{2,3},{3,0},{4,5},{5,6},{6,7},{7,4},{8,9},{9,10},{10,1... | collective-permute-start | bytes 294920 | tf_op jit(solution)/shard_map/ppermute | solution.py:472
  28.4 5.5 %halo_terms.3 = bf16[1536,128]{1,0:T(8,128)(2,1)S(1)} custom-call(s32[32,16]{1,0:T(8,128)S(1)} %slice_convert_fusion.lists, f32[128,128]{1,0:T(8,128)S(1)} %collective-permute-done.9.held, bf16[24,256,128]{2,1,0:T(8,128)(2,1)S(1)} %get-tuple-element.15.v_ref, bf16[24,16,256]{2,1,0:T(8,128)(2,1)S(1)} %get-tuple-element.16.f_ref, ...), custom_call_target="tpu_custom_call" | custom-call | flops 6000000000 | bytes 3000000 | tf_op jit(solution)/shard_map/halo_terms/pallas_call | solution.py:486
  33.9 3.1 %collective-permute-start.10 = (bf16[1536,128]{1,0:T(8,128)(2,1)S(1)}, bf16[1536,128]{1,0:T(8,128)(2,1)S(1)}, u32[]{:S(2)}, u32[]{:S(2)}) collective-permute-start(bf16[1536,128]{1,0:T(8,128)(2,1)S(1)} %halo_terms.3), channel_id=1, source_target_pairs={{1,0},{2,1},{3,2},{4,3},{5,4},{6,5},{7,6},{8,7},{9,8},{10,9},{11,1... | collective-permute-start | bytes 1179656 | tf_op jit(solution)/shard_map/ppermute | solution.py:502
  37.0 0.0 collective-permute-done.5
  37.0 0.0 collective-permute-done.6
  37.1 0.0 collective-permute-done.7
  37.1 0.1 collective-permute-start.13
  37.2 3.7 %collective-permute-start.12 = (bf16[1536,128]{1,0:T(8,128)(2,1)S(1)}, bf16[1536,128]{1,0:T(8,128)(2,1)S(1)}, u32[]{:S(2)}, u32[]{:S(2)}) collective-permute-start(bf16[1536,128]{1,0:T(8,128)(2,1)S(1)} %constant_dynamic-update-slice_fusion.after.y0), channel_id=1, source_target_pairs={{0,8},{1,9},{2,10},{3,11},{4,12},{5,13},{6,14},{7,15},{8,0},{9,1},... | collective-permute-start | bytes 1179656 | tf_op jit(solution)/shard_map/ppermute | solution.py:472
  40.9 0.9 collective-permute-start.11
  41.7 6.2 %halo_terms.2.after = bf16[1536,128]{1,0:T(8,128)(2,1)S(1)} custom-call(s32[32,16]{1,0:T(8,128)S(1)} %slice_convert_fusion.1.lists, f32[128,128]{1,0:T(8,128)S(1)} %collective-permute-done.held, bf16[24,256,128]{2,1,0:T(8,128)(2,1)S(1)} %get-tuple-element.15.v_ref, bf16[24,16,256]{2,1,0:T(8,128)(2,1)S(1)} %get-tuple-element.16.f_ref, ...), custom_call_target="tpu_custom_call" | custom-call | flops 6000000000 | bytes 3000000 | tf_op jit(solution)/shard_map/halo_terms/pallas_call | solution.py:486
  47.9 1.9 %collective-permute-start.8 = (bf16[1536,128]{1,0:T(8,128)(2,1)S(1)}, bf16[1536,128]{1,0:T(8,128)(2,1)S(1)}, u32[]{:S(2)}, u32[]{:S(2)}) collective-permute-start(bf16[1536,128]{1,0:T(8,128)(2,1)S(1)} %halo_terms.2.after), channel_id=1, source_target_pairs={{0,1},{1,2},{2,3},{3,4},{4,5},{5,6},{6,7},{7,8},{8,9},{9,10},{10,1... | collective-permute-start | bytes 1179656 | tf_op jit(solution)/shard_map/ppermute | solution.py:504
  49.8 0.0 copy-start
  49.9 0.0 copy-start.1
  49.9 4.6 %own_terms.1 = (f32[7,256,128]{2,1,0:T(8,128)S(1)}, bf16[17,256,16]{2,1,0:T(8,128)(2,1)S(1)}) custom-call(s32[32,16]{1,0:T(8,128)S(1)} %get-tuple-element.13.lists, f32[128,128]{1,0:T(8,128)S(1)} %get-tuple-element.14.held, bf16[24,256,128]{2,1,0:T(8,128)(2,1)S(1)} %get-tuple-element.15.v_ref, bf16[24,16,256]{2,1,0:T(8,128)(2,1)S(1)} %get-tuple-element.16.f_ref, ...), custom_call_target="tpu_custom_call" | custom-call | flops 5000000000 | bytes 3000000 | tf_op jit(solution)/shard_map/own_terms/pallas_call | solution.py:506
  54.5 10.5 %collective-permute-done.13.y3 = bf16[1536,128]{1,0:T(8,128)(2,1)S(1)} collective-permute-done((bf16[1536,128]{1,0:T(8,128)(2,1)S(1)}, bf16[1536,128]{1,0:T(8,128)(2,1)S(1)}, u32[]{:S(2)}, u32[]{:S(2)}) %collective-permute-start.13) | collective-permute-done | bytes 393248 | tf_op jit(solution)/shard_map/ppermute | solution.py:472
  65.0 0.0 collective-permute-done.12.y2
  65.0 0.0 collective-permute-done.11.y1
  65.0 0.0 copy-done
  65.0 10.6 %top_terms.1.top = f32[2,16,2048]{2,1,0:T(8,128)S(1)} custom-call(s32[16,12]{1,0:T(8,128)S(1)} %copy-done, s32[16]{0:T(128)S(1)} %copy-done.1, bf16[17,256,16]{2,1,0:T(8,128)(2,1)S(1)} %get-tuple-element.20.a_all.a_ref, bf16[1536,128]{1,0:T(8,128)(2,1)S(1)} %constant_dynamic-update-slice_fusion.after.y0, bf16[1536,128]{1,0:T(8,128)(2,1)S(1)} %collective-permute-done.11.y1, ...), custom_call_target="tpu_custom_call" | custom-call | flops 6000000000 | bytes 3000000 | tf_op jit(solution)/shard_map/top_terms/pallas_call | solution.py:524
  75.6 0.0 collective-permute-done.10.halo_r
  75.6 0.0 collective-permute-done.8.halo_l
  75.6 7.7 %node_terms.1 = f32[2,4,16,4096]{3,2,1,0:T(8,128)S(1)} custom-call(s32[32,16]{1,0:T(8,128)S(1)} %get-tuple-element.13.lists, f32[7,256,128]{2,1,0:T(8,128)S(1)} %get-tuple-element.19.own, bf16[17,256,16]{2,1,0:T(8,128)(2,1)S(1)} %get-tuple-element.20.a_all.a_ref, bf16[1536,128]{1,0:T(8,128)(2,1)S(1)} %collective-permute-done.8.halo_l, ...), custom_call_target="tpu_custom_call" | custom-call | flops 6000000000 | bytes 3000000 | tf_op jit(solution)/shard_map/node_terms/pallas_call | solution.py:542
  83.3 0.1 slice_bitcast_fusion
  83.4 0.1 collective-permute-start.14
  83.5 2.6 %collective-permute-done.14 = f32[4,16,4096]{2,1,0:T(8,128)S(1)} collective-permute-done((f32[4,16,4096]{2,1,0:T(8,128)S(1)}, f32[4,16,4096]{2,1,0:T(8,128)S(1)}, u32[]{:S(2)}, u32[]{:S(2)}) %collective-permute-start.14) | collective-permute-done | bytes 1048608 | tf_op jit(solution)/shard_map/ppermute | solution.py:557
  86.1 0.1 fusion.10
  86.3 0.1 collective-permute-start.15
  86.4 3.0 %collective-permute-start.17 = (bf16[16,4096]{1,0:T(8,128)(2,1)S(1)}, bf16[16,4096]{1,0:T(8,128)(2,1)S(1)}, u32[]{:S(2)}, u32[]{:S(2)}) collective-permute-start(bf16[16,4096]{1,0:T(8,128)(2,1)S(1)} %get-tuple-element.26), channel_id=1, source_target_pairs={{0,64},{16,80},{32,96},{48,112},{64,0},{80,16},{96,32},{112,48},{1... | collective-permute-start | bytes 393224 | tf_op jit(solution)/shard_map/ppermute | solution.py:560
  89.4 1.2 %collective-permute-start.16 = (bf16[16,4096]{1,0:T(8,128)(2,1)S(1)}, bf16[16,4096]{1,0:T(8,128)(2,1)S(1)}, u32[]{:S(2)}, u32[]{:S(2)}) collective-permute-start(bf16[16,4096]{1,0:T(8,128)(2,1)S(1)} %get-tuple-element.27), channel_id=1, source_target_pairs={{0,96},{16,112},{32,0},{48,16},{64,32},{80,48},{96,64},{112,80},{1... | collective-permute-start | bytes 393224 | tf_op jit(solution)/shard_map/ppermute | solution.py:560
  90.7 5.3 %collective-permute-done.15 = bf16[16,4096]{1,0:T(8,128)(2,1)S(1)} collective-permute-done((bf16[16,4096]{1,0:T(8,128)(2,1)S(1)}, bf16[16,4096]{1,0:T(8,128)(2,1)S(1)}, u32[]{:S(2)}, u32[]{:S(2)}) %collective-permute-start.15) | collective-permute-done | bytes 131104 | tf_op jit(solution)/shard_map/ppermute | solution.py:560
  95.9 0.0 collective-permute-done.17
  95.9 0.6 collective-permute-done.16
  96.5 0.8 fusion.4
  (12 shorter events, 0.2 us)
Async XLA Ops:
  7.5 8.3 %collective-permute-start.9 = (f32[128,128]{1,0:T(8,128)S(1)}, f32[128,128]{1,0:T(8,128)S(1)}, u32[]{:S(2)}, u32[]{:S(2)}) collective-permute-start(f32[128,128]{1,0:T(8,128)S(1)} %get-tuple-element.14.held), channel_id=1, source_target_pairs={{0,1},{1,2},{2,3},{3,4},{4,5},{5,6},{6,7},{7,8},{8,9},{9,10},{10,1... | collective-permute-start | bytes 196616 | tf_op jit(solution)/shard_map/ppermute | solution.py:461
  11.4 11.3 %collective-permute-start = (f32[128,128]{1,0:T(8,128)S(1)}, f32[128,128]{1,0:T(8,128)S(1)}, u32[]{:S(2)}, u32[]{:S(2)}) collective-permute-start(f32[128,128]{1,0:T(8,128)S(1)} %get-tuple-element.14.held), channel_id=1, source_target_pairs={{1,0},{2,1},{3,2},{4,3},{5,4},{6,5},{7,6},{8,7},{9,8},{10,9},{11,1... | collective-permute-start | bytes 196616 | tf_op jit(solution)/shard_map/ppermute | solution.py:462
  15.5 1.4 %collective-permute-start.1 = (bf16[4,96,128]{2,1,0:T(8,128)(2,1)S(1)}, bf16[4,96,128]{2,1,0:T(8,128)(2,1)S(1)}, u32[]{:S(2)}, u32[]{:S(2)}) collective-permute-start(bf16[4,96,128]{2,1,0:T(8,128)(2,1)S(1)} %get-tuple-element.18), channel_id=1, source_target_pairs={{0,16},{16,0},{32,48},{48,32},{64,80},{80,64},{96,112},{112,96},{1... | collective-permute-start | bytes 294920 | tf_op jit(solution)/shard_map/ppermute | solution.py:477
  16.9 5.8 %collective-permute-start.2 = (bf16[96,128]{1,0:T(8,128)(2,1)S(1)}, bf16[96,128]{1,0:T(8,128)(2,1)S(1)}, u32[]{:S(2)}, u32[]{:S(2)}) collective-permute-start(bf16[96,128]{1,0:T(8,128)(2,1)S(1)} %get-tuple-element.30), channel_id=1, source_target_pairs={{0,32},{16,48},{32,64},{48,80},{64,96},{80,112},{96,0},{112,16},{1... | collective-permute-start | bytes 73736 | tf_op jit(solution)/shard_map/ppermute | solution.py:480
  18.5 5.3 %collective-permute-start.4 = (bf16[96,128]{1,0:T(8,128)(2,1)S(1)}, bf16[96,128]{1,0:T(8,128)(2,1)S(1)}, u32[]{:S(2)}, u32[]{:S(2)}) collective-permute-start(bf16[96,128]{1,0:T(8,128)(2,1)S(1)} %get-tuple-element.31), channel_id=1, source_target_pairs={{0,64},{16,80},{32,96},{48,112},{64,0},{80,16},{96,32},{112,48},{1... | collective-permute-start | bytes 73736 | tf_op jit(solution)/shard_map/ppermute | solution.py:480
  21.2 3.8 %collective-permute-start.3 = (bf16[96,128]{1,0:T(8,128)(2,1)S(1)}, bf16[96,128]{1,0:T(8,128)(2,1)S(1)}, u32[]{:S(2)}, u32[]{:S(2)}) collective-permute-start(bf16[96,128]{1,0:T(8,128)(2,1)S(1)} %get-tuple-element.32), channel_id=1, source_target_pairs={{0,96},{16,112},{32,0},{48,16},{64,32},{80,48},{96,64},{112,80},{1... | collective-permute-start | bytes 73736 | tf_op jit(solution)/shard_map/ppermute | solution.py:480
  25.1 12.0 %collective-permute-start.7 = (bf16[384,128]{1,0:T(8,128)(2,1)S(1)}, bf16[384,128]{1,0:T(8,128)(2,1)S(1)}, u32[]{:S(2)}, u32[]{:S(2)}) collective-permute-start(bf16[384,128]{1,0:T(8,128)(2,1)S(1)} %pad_maximum_fusion.after), channel_id=1, source_target_pairs={{0,3},{1,0},{2,1},{3,2},{4,7},{5,4},{6,5},{7,6},{8,11},{9,8},{10,9... | collective-permute-start | bytes 294920 | tf_op jit(solution)/shard_map/ppermute | solution.py:472
  27.1 10.0 %collective-permute-start.6 = (bf16[384,128]{1,0:T(8,128)(2,1)S(1)}, bf16[384,128]{1,0:T(8,128)(2,1)S(1)}, u32[]{:S(2)}, u32[]{:S(2)}) collective-permute-start(bf16[384,128]{1,0:T(8,128)(2,1)S(1)} %pad_maximum_fusion.after), channel_id=1, source_target_pairs={{0,2},{1,3},{2,0},{3,1},{4,6},{5,7},{6,4},{7,5},{8,10},{9,11},{10,... | collective-permute-start | bytes 294920 | tf_op jit(solution)/shard_map/ppermute | solution.py:472
  27.1 9.9 %collective-permute-start.5 = (bf16[384,128]{1,0:T(8,128)(2,1)S(1)}, bf16[384,128]{1,0:T(8,128)(2,1)S(1)}, u32[]{:S(2)}, u32[]{:S(2)}) collective-permute-start(bf16[384,128]{1,0:T(8,128)(2,1)S(1)} %pad_maximum_fusion.after), channel_id=1, source_target_pairs={{0,1},{1,2},{2,3},{3,0},{4,5},{5,6},{6,7},{7,4},{8,9},{9,10},{10,1... | collective-permute-start | bytes 294920 | tf_op jit(solution)/shard_map/ppermute | solution.py:472
  33.9 41.7 %collective-permute-start.10 = (bf16[1536,128]{1,0:T(8,128)(2,1)S(1)}, bf16[1536,128]{1,0:T(8,128)(2,1)S(1)}, u32[]{:S(2)}, u32[]{:S(2)}) collective-permute-start(bf16[1536,128]{1,0:T(8,128)(2,1)S(1)} %halo_terms.3), channel_id=1, source_target_pairs={{1,0},{2,1},{3,2},{4,3},{5,4},{6,5},{7,6},{8,7},{9,8},{10,9},{11,1... | collective-permute-start | bytes 1179656 | tf_op jit(solution)/shard_map/ppermute | solution.py:502
  37.1 27.9 %collective-permute-start.13 = (bf16[1536,128]{1,0:T(8,128)(2,1)S(1)}, bf16[1536,128]{1,0:T(8,128)(2,1)S(1)}, u32[]{:S(2)}, u32[]{:S(2)}) collective-permute-start(bf16[1536,128]{1,0:T(8,128)(2,1)S(1)} %constant_dynamic-update-slice_fusion.after.y0), channel_id=1, source_target_pairs={{0,12},{1,13},{2,14},{3,15},{4,0},{5,1},{6,2},{7,3},{8,4},{9,5},{1... | collective-permute-start | bytes 1179656 | tf_op jit(solution)/shard_map/ppermute | solution.py:472
  37.2 27.8 %collective-permute-start.12 = (bf16[1536,128]{1,0:T(8,128)(2,1)S(1)}, bf16[1536,128]{1,0:T(8,128)(2,1)S(1)}, u32[]{:S(2)}, u32[]{:S(2)}) collective-permute-start(bf16[1536,128]{1,0:T(8,128)(2,1)S(1)} %constant_dynamic-update-slice_fusion.after.y0), channel_id=1, source_target_pairs={{0,8},{1,9},{2,10},{3,11},{4,12},{5,13},{6,14},{7,15},{8,0},{9,1},... | collective-permute-start | bytes 1179656 | tf_op jit(solution)/shard_map/ppermute | solution.py:472
  40.9 24.2 %collective-permute-start.11 = (bf16[1536,128]{1,0:T(8,128)(2,1)S(1)}, bf16[1536,128]{1,0:T(8,128)(2,1)S(1)}, u32[]{:S(2)}, u32[]{:S(2)}) collective-permute-start(bf16[1536,128]{1,0:T(8,128)(2,1)S(1)} %constant_dynamic-update-slice_fusion.after.y0), channel_id=1, source_target_pairs={{0,4},{1,5},{2,6},{3,7},{4,8},{5,9},{6,10},{7,11},{8,12},{9,13},{1... | collective-permute-start | bytes 1179656 | tf_op jit(solution)/shard_map/ppermute | solution.py:472
  47.9 27.7 %collective-permute-start.8 = (bf16[1536,128]{1,0:T(8,128)(2,1)S(1)}, bf16[1536,128]{1,0:T(8,128)(2,1)S(1)}, u32[]{:S(2)}, u32[]{:S(2)}) collective-permute-start(bf16[1536,128]{1,0:T(8,128)(2,1)S(1)} %halo_terms.2.after), channel_id=1, source_target_pairs={{0,1},{1,2},{2,3},{3,4},{4,5},{5,6},{6,7},{7,8},{8,9},{9,10},{10,1... | collective-permute-start | bytes 1179656 | tf_op jit(solution)/shard_map/ppermute | solution.py:504
  49.8 15.2 %copy-start = (s32[16,12]{1,0:T(8,128)S(1)}, s32[16,12]{1,0:T(8,128)}, u32[]{:S(2)}) copy-start(s32[16,12]{1,0:T(8,128)} %listed.1) | copy-start | bytes 2308
  49.9 15.2 %copy-start.1 = (s32[16]{0:T(128)S(1)}, s32[16]{0:T(128)}, u32[]{:S(2)}) copy-start(s32[16]{0:T(128)} %counts.1) | copy-start | bytes 196
  83.4 2.7 %collective-permute-start.14 = (f32[4,16,4096]{2,1,0:T(8,128)S(1)}, f32[4,16,4096]{2,1,0:T(8,128)S(1)}, u32[]{:S(2)}, u32[]{:S(2)}) collective-permute-start(f32[4,16,4096]{2,1,0:T(8,128)S(1)} %slice_bitcast_fusion), channel_id=1, source_target_pairs={{0,16},{16,0},{32,48},{48,32},{64,80},{80,64},{96,112},{112,96},{1... | collective-permute-start | bytes 3145736 | tf_op jit(solution)/shard_map/ppermute | solution.py:557
  86.3 9.6 %collective-permute-start.15 = (bf16[16,4096]{1,0:T(8,128)(2,1)S(1)}, bf16[16,4096]{1,0:T(8,128)(2,1)S(1)}, u32[]{:S(2)}, u32[]{:S(2)}) collective-permute-start(bf16[16,4096]{1,0:T(8,128)(2,1)S(1)} %get-tuple-element.25), channel_id=1, source_target_pairs={{0,32},{16,48},{32,64},{48,80},{64,96},{80,112},{96,0},{112,16},{1... | collective-permute-start | bytes 393224 | tf_op jit(solution)/shard_map/ppermute | solution.py:560
  86.4 9.5 %collective-permute-start.17 = (bf16[16,4096]{1,0:T(8,128)(2,1)S(1)}, bf16[16,4096]{1,0:T(8,128)(2,1)S(1)}, u32[]{:S(2)}, u32[]{:S(2)}) collective-permute-start(bf16[16,4096]{1,0:T(8,128)(2,1)S(1)} %get-tuple-element.26), channel_id=1, source_target_pairs={{0,64},{16,80},{32,96},{48,112},{64,0},{80,16},{96,32},{112,48},{1... | collective-permute-start | bytes 393224 | tf_op jit(solution)/shard_map/ppermute | solution.py:560
  89.4 7.1 %collective-permute-start.16 = (bf16[16,4096]{1,0:T(8,128)(2,1)S(1)}, bf16[16,4096]{1,0:T(8,128)(2,1)S(1)}, u32[]{:S(2)}, u32[]{:S(2)}) collective-permute-start(bf16[16,4096]{1,0:T(8,128)(2,1)S(1)} %get-tuple-element.27), channel_id=1, source_target_pairs={{0,96},{16,112},{32,0},{48,16},{64,32},{80,48},{96,64},{112,80},{1... | collective-permute-start | bytes 393224 | tf_op jit(solution)/shard_map/ppermute | solution.py:560
where the time goes:
time: 96.8 us; the launch traced here: 97.3 us
  Pallas kernels  42 us (43%)
  starting transfers between devices  31.1 us (32%)
  waiting for transfers between devices  22.7 us (23%)
  other arithmetic  0.98 us (1%)
    pallas_call x2, Pallas kernels, halo(): pl.pallas_call(functools.partial(halo_kernel, base), out_shape=jax.ShapeD...  11.7 us
    pallas_call x1, Pallas kernels, shards(): pl.pallas_call(top_kernel, out_shape=jax.ShapeDtypeStruct((2, 16, half *...  10.6 us
    ppermute x6, waiting for transfers between devices, others(): return [lax.ppermute(x, axis, shifts[d]) for d in (1, 3, 2)]  10.5 us
    ppermute x6, starting transfers between devices, others(): return [lax.ppermute(x, axis, shifts[d]) for d in (1, 3, 2)]  7.89 us
    pallas_call x1, Pallas kernels, shards(): pl.pallas_call(node_kernel, out_shape=jax.ShapeDtypeStruct((2, 4, 16, TL_...  7.66 us
    pallas_call x1, Pallas kernels, shards(): pl.pallas_call(leaf_kernel, out_shape=(OUT((24, 256, Q), bf16), OUT((24,...  7.51 us
    ppermute x3, waiting for transfers between devices, shards(): lax.ppermute(pair[d].astype(bf16), 'src', xshift[d]).astype(f32)  5.84 us
    ppermute x3, starting transfers between devices, shards(): lax.ppermute(top_pair[d].astype(bf16), 'src', xshift[d]).astype(f32)  5.74 us
  transfers between devices with their start and end apart: 18, of which 8 were waited for; matrix products, arithmetic and copies ran while one was open for 0% of the time, Pallas kernels for 28%

commit v1 on v0

--- a/solution.py
+++ b/solution.py
@@ -16,7 +16,7 @@
 WIN = 6
 KF = 16
 LN2 = 0.6931471805599453
-SCALE = 2.0 / LN2
+SCALE = 2.0
 GROUP = 16
 TAIL = 4
 VMEM = pltpu.VMEM
@@ -27,11 +27,12 @@
 NEAR_N, FAR_N, NODE_N = 24, 25, 26
 LIST_ROWS = 32
 POINT_ROWS = 96
+HELD = 3 * POINT_ROWS + LIST_ROWS
 TRASH = 16
 PART = 384
 BIG = 60
 OUT = pltpu.VMEM
-HALO_COST = 6e9
+HALO_COST = 1e9
 OWN_COST = 5e9
 NODE_COST = 6e9
 TOP_COST = 6e9
@@ -69,7 +70,7 @@
 def matern(w):
     w = jnp.maximum(w, 1e-12)
     u = w * lax.rsqrt(w)
-    return ((1.0 + LN2 * u) * jnp.exp2(-u)).astype(bf16)
+    return ((1.0 + u) * jnp.exp2(u * (-1.0 / LN2))).astype(bf16)
 
 
 def take(row, index):
@@ -93,16 +94,16 @@
     src = lax.axis_index("src")
     tgt = lax.axis_index("tgt")
     start = jnp.clip(2 * src - 2, 0, TL_J - WIN)
-    return src, src >> 1, src & 1, tgt >> 2, tgt & 3, start
+    return src, src >> 1, src & 1, tgt, start
 
 
 def leaf_kernel(
     idx_h, piv_h, npiv_h, tpiv_h, pts_h, vals_h, proj_h, nproj_h, tproj_h,
     tpts_h, near_h, far_h, node_h, nearn_h, farn_h, noden_h,
     v_out, f_out, n_out, t_out, held_out, lists_out, idx, piv, npiv, tpiv, pts, vals, proj, nproj, tproj,
-    tpts, near, far, node, nearn, farn, noden, wide, gathered, fs, ns, idx_s, sems,
+    tpts, near, far, node, nearn, farn, noden, wide, gathered, fs, ns, hf, lf, idx_s, sems,
 ):
-    src, chip, _, _, _, _ = place()
+    src, chip, _, _, _ = place()
     rows = vals.shape[0]
     moves = [(pts_h, pts), (idx_h, idx), (piv_h, piv), (npiv_h, npiv), (tpiv_h, tpiv), (vals_h, vals),
              (proj_h, proj), (nproj_h, nproj), (tproj_h, tproj), (tpts_h, tpts), (near_h, near), (far_h, far),
@@ -156,7 +157,9 @@
     step = POINT_ROWS // 3
     for c in range(3):
         for k in range(step):
-            held_out[step * c + k : step * c + k + 1, :] = tpts[c : c + 1, 128 * k : 128 * k + 128]
+            hf[step * c + k : step * c + k + 1, :] = tpts[c : c + 1, 128 * k : 128 * k + 128]
+    for k, piece in enumerate(split3(hf[...])):
+        held_out[POINT_ROWS * k : POINT_ROWS * k + POINT_ROWS, :] = piece.astype(bf16)
     lists_out[...] = jnp.zeros_like(lists_out)
     lists_out[NEAR_AT : FAR_AT, :] = near[0]
     for e in range(NODE_AT - FAR_AT):
@@ -165,8 +168,9 @@
     lists_out[NEAR_N : NEAR_N + 1, :] = nearn[...]
     lists_out[FAR_N : FAR_N + 1, :] = farn[...]
     lists_out[NODE_N : NODE_N + 1, :] = noden[...]
-    held_out[POINT_ROWS:, :] = jnp.zeros((LIST_ROWS, 128), f32)
-    held_out[POINT_ROWS:, :TL_J] = lists_out[...].astype(f32)
+    lf[...] = jnp.zeros_like(lf)
+    lf[:, :TL_J] = lists_out[...].astype(f32)
+    held_out[3 * POINT_ROWS :, :] = lf[...].astype(bf16)
     copies[5].wait()
 
     def widen(k, _):
@@ -205,9 +209,11 @@
             t_out[at, 48 * half + 32 : 48 * half + 48, :] = lanes(pieces, half)
 
 
-def target_rows(held, first, count, fa):
+def target_rows(held, base, hf, first, count, fa):
     step = TL_J * TLEAF // 128
-    rows = features([centred(held[pl.ds(step * c + first, count), :]) for c in range(3)], False)
+    pieces = [held[base + POINT_ROWS * k : base + POINT_ROWS * (k + 1), :].astype(f32) for k in range(3)]
+    hf[...] = pieces[0] + pieces[1] + pieces[2]
+    rows = features([centred(hf[pl.ds(step * c + first, count), :]) for c in range(3)], False)
     for f, row in enumerate(rows):
         for k in range(count):
             fa[f : f + 1, 128 * k : 128 * k + 128] = row[k : k + 1, :]
@@ -245,10 +251,10 @@
     lax.fori_loop(0, (n - done + TAIL - 1) // TAIL, small, 0)
 
 
-def leaf_pairs(pairs, lists, start, base):
+def leaf_pairs(pairs, lists, start, base, live):
     def target(t, n):
         leaf = start + t
-        near, far = lists[NEAR_N, leaf], lists[FAR_N, leaf]
+        near, far = live * lists[NEAR_N, leaf], live * lists[FAR_N, leaf]
         for e in range(FAR_AT):
             v = lists[NEAR_AT + e, leaf] - base
             pairs[n] = 64 * v + t
@@ -271,38 +277,42 @@
     lax.fori_loop(0, acc.shape[0], one, 0)
 
 
-def halo_kernel(base, lists, held, v_ref, f_ref, after, out, fa, a_ref, acc, pairs):
-    start = place()[5]
+def halo_kernel(base, lists, held, v_ref, f_ref, after, out, hf, fa, a_ref, acc, pairs):
+    _, _, _, tgt, start = place()
+    live = (tgt > 0 if base else tgt < 15).astype(jnp.int32)
     clear(acc)
-    target_rows(held, 2 * start, 2 * WIN, fa)
+    target_rows(held, PART, hf, 2 * start, 2 * WIN, fa)
     set_targets(fa, a_ref, WIN)
-    n = leaf_pairs(pairs, lists, start, base)
+    n = leaf_pairs(pairs, lists, start, base, live)
     run_pairs(pairs, n, WIN, a_ref, f_ref, lambda s: v_ref[s], acc)
     for t in range(WIN):
         out[t * TLEAF : (t + 1) * TLEAF, :] = acc[t].astype(bf16)
 
 
-def own_kernel(lists, held, v_ref, f_ref, after, out, a_all, fa, a_ref, pairs):
-    start = place()[5]
+def own_kernel(lists, held, v_ref, f_ref, after, out, a_all, hf, fa, a_ref, pairs):
+    start = place()[4]
     clear(out)
-    target_rows(held, 0, 2 * TL_J, fa)
+    target_rows(held, 0, hf, 0, 2 * TL_J, fa)
     set_targets(fa, a_all, TL_J)
     for t in range(WIN):
         a_ref[t] = a_all[start + t]
     a_ref[WIN] = jnp.zeros((TLEAF, KF), bf16)
-    n = leaf_pairs(pairs, lists, start, SL)
+    n = leaf_pairs(pairs, lists, start, SL, 1)
     run_pairs(pairs, n, WIN, a_ref, f_ref, lambda s: v_ref[s], out)
 
 
-def slot_of(column, row, plane):
-    return 4 * ((row - (column >> 2)) & 3) + ((plane - (column & 3)) & 3)
+def slot_of(column, tgt):
+    back = (tgt - column) & 15
+    near = back & 3
+    far = jnp.where(near == 3, (back >> 2) + 1, back >> 2) & 3
+    return 4 * far + near
 
 
 def node_kernel(
     lists, own, a_ref, halo_l, halo_r, top, y0, y1, y2, y3,
     out, acc, ys, f_ref, pairs, sems,
 ):
-    _, chip, core, row, plane, start = place()
+    _, chip, core, tgt, start = place()
     copies = [pltpu.make_async_copy(y, ys.at[k], sems.at[k]) for k, y in enumerate((y0, y1, y2, y3))]
     for copy in copies:
         copy.start()
@@ -313,7 +323,7 @@
 
     def target(t, n):
         for e in range(NEAR_N - NODE_AT):
-            pairs[n + e] = 32 * slot_of(lists[NODE_AT + e, t], row, plane) + t
+            pairs[n + e] = 32 * slot_of(lists[NODE_AT + e, t], tgt) + t
         return n + lists[NODE_N, t]
 
     n = lax.fori_loop(0, TL_J, target, 0)
@@ -345,10 +355,10 @@
             out[k, 0, :, pl.ds(at, TLEAF)] += top[k, :, t * TLEAF : (t + 1) * TLEAF]
 
 
-def top_pairs(pairs, listed, counts, row, plane, first, count):
+def top_pairs(pairs, listed, counts, tgt, first, count):
     def target(t, n):
         for e in range(listed.shape[1]):
-            pairs[n + e] = 32 * slot_of(listed[first + t, e], row, plane) + t
+            pairs[n + e] = 32 * slot_of(listed[first + t, e], tgt) + t
         return n + counts[first + t]
 
     return lax.fori_loop(0, count, target, 0)
@@ -356,7 +366,7 @@
 
 def top_kernel(listed, counts, a_all, y0, y1, y2, y3, out, f_ref, v_ref, a_ref, acc, pw, fw, pairs):
     count = TL_J // 2
-    _, _, core, row, plane, _ = place()
+    _, _, core, tgt, _ = place()
     first = core * count
     for dy, ys in enumerate((y0, y1, y2, y3)):
         for dz in range(4):
@@ -379,7 +389,7 @@
         a_ref[t] = a_all[first + t]
     a_ref[count] = jnp.zeros((TLEAF, KF), bf16)
     clear(acc)
-    n = top_pairs(pairs, listed, counts, row, plane, first, count)
+    n = top_pairs(pairs, listed, counts, tgt, first, count)
     run_pairs(pairs, n, count, a_ref, f_ref, lambda s: v_ref[s], acc)
     for t in range(count):
         block = acc[t].T
@@ -421,7 +431,7 @@
             OUT((24, KF, 256), bf16),
             OUT((288, Q), bf16),
             OUT((4, 96, 128), bf16),
-            OUT((POINT_ROWS + LIST_ROWS, 128), f32),
+            OUT((HELD, 128), bf16),
             OUT((LIST_ROWS, TL_J), jnp.int32),
         ),
         in_specs=[anywhere] * 16,
@@ -447,6 +457,8 @@
             VMEM((4096, Q), f32),
             VMEM((24, KF, 256), f32),
             VMEM((KF, 256), f32),
+            VMEM((POINT_ROWS, 128), f32),
+            VMEM((LIST_ROWS, 128), f32),
             pltpu.SMEM((4096,), jnp.int32),
             pltpu.SemaphoreType.DMA((24,)),
         ],
@@ -458,13 +470,9 @@
       node_list.transpose(0, 2, 1), near_count, far_count, node_count)
     forward = shift("tgt", 16, lambda i: i + 1)
     backward = shift("tgt", 16, lambda i: i - 1)
-    held_l = lax.ppermute(held, "tgt", forward)
-    held_r = lax.ppermute(held, "tgt", backward)
-    lists_l = held_l[POINT_ROWS:, :TL_J].astype(jnp.int32)
-    lists_r = held_r[POINT_ROWS:, :TL_J].astype(jnp.int32)
-
-    zshift = [shift("tgt", 16, lambda i, d=d: (i // 4) * 4 + (i % 4 + d) % 4) for d in range(4)]
-    yshift = [shift("tgt", 16, lambda i, d=d: ((i // 4 + d) % 4) * 4 + i % 4) for d in range(4)]
+
+    around = {d: shift("tgt", 16, lambda i, d=d: (i + d) % 16) for d in (1, -1, 2, 4, 8, 12)}
+    yshift = [None, around[4], around[8], around[12]]
     xshift = [shift("src", 8, lambda i, d=d: (i + 2 * d) % 8) for d in range(4)]
     cores = shift("src", 8, lambda i: i ^ 1)
 
@@ -479,7 +487,13 @@
     for d in (1, 3, 2):
         top_sum = top_sum + lax.ppermute(top_pair[d].astype(bf16), "src", xshift[d]).astype(f32)
     parts = jnp.concatenate([node_own, top_sum.astype(bf16)], axis=0)
-    bundle = jnp.concatenate(in_order(parts, others(parts, "tgt", zshift)), axis=0)
+    wide = jnp.concatenate([parts, held], axis=0)
+    from_l = lax.ppermute(wide, "tgt", around[1])
+    from_r = lax.ppermute(wide, "tgt", around[-1])
+    from_2 = lax.ppermute(parts, "tgt", around[2])
+    lists_l = from_l[PART + 3 * POINT_ROWS :, :TL_J].astype(jnp.int32)
+    lists_r = from_r[PART + 3 * POINT_ROWS :, :TL_J].astype(jnp.int32)
+    bundle = jnp.concatenate([parts, from_l[:PART], from_2, from_r[:PART]], axis=0)
     ys = in_order(bundle, others(bundle, "tgt", yshift))
 
     def halo(base, lists_of, held_of, after):
@@ -489,6 +503,7 @@
             in_specs=[smem] + whole(3) + [anywhere],
             out_specs=pl.BlockSpec(memory_space=VMEM),
             scratch_shapes=[
+                VMEM((POINT_ROWS, 128), f32),
                 VMEM((KF, WIN * TLEAF), f32),
                 VMEM((WIN + 1, TLEAF, KF), bf16),
                 VMEM((WIN + 1, TLEAF, Q), f32),
@@ -497,11 +512,6 @@
             cost_estimate=cost(HALO_COST, 3e6),
             name="halo_terms",
         )(lists_of, held_of, v_all, f_all, after)
-
-    to_l = halo(16, lists_l, held_l, parts)
-    got_r = lax.ppermute(to_l, "tgt", backward)
-    to_r = halo(0, lists_r, held_r, bundle)
-    got_l = lax.ppermute(to_r, "tgt", forward)
 
     own, a_all = pl.pallas_call(
         own_kernel,
@@ -512,13 +522,19 @@
         in_specs=[smem] + whole(3) + [anywhere],
         out_specs=tuple(whole(2)),
         scratch_shapes=[
+            VMEM((POINT_ROWS, 128), f32),
             VMEM((KF, TL_J * TLEAF), f32),
             VMEM((WIN + 1, TLEAF, KF), bf16),
         ] + pair_scratch(),
         compiler_params=params(24),
         cost_estimate=cost(OWN_COST, 3e6),
         name="own_terms",
-    )(lists, held, v_all, f_all, to_r)
+    )(lists, held, v_all, f_all, wide)
+
+    to_l = halo(16, lists_l, from_l, own)
+    got_r = lax.ppermute(to_l, "tgt", backward)
+    to_r = halo(0, lists_r, from_r, to_l)
+    got_l = lax.ppermute(to_r, "tgt", forward)
 
     half = TL_J // 2
     top_term = pl.pallas_call(

time: 96.8 us -> 86.3 us (0.89)
  starting transfers between devices: 31.1 us -> 26.6 us
  Pallas kernels: 42 us -> 38.6 us
  waiting for transfers between devices: 22.7 us -> 19.5 us
    ppermute x6 -> x3, waiting for transfers between devices: 10.5 us -> 0.87 us  [others(): return [lax.ppermute(x, axis, shifts[d]) for d in (1, 3, 2)]]
    ppermute x1, waiting for transfers between devices: 0.01 us -> 5.36 us  [shards(): got_l = lax.ppermute(to_r, 'tgt', forward)]
    pallas_call x1, Pallas kernels: 10.6 us -> 7.65 us  [shards(): pl.pallas_call(top_kernel, out_shape=jax.ShapeDtypeStruct((2, 16, half *...]
    ppermute x6 -> x3, starting transfers between devices: 7.89 us -> 5.41 us  [others(): return [lax.ppermute(x, axis, shifts[d]) for d in (1, 3, 2)]]
    pallas_call x2, Pallas kernels: 11.7 us -> 9.49 us  [halo(): pl.pallas_call(functools.partial(halo_kernel, base), out_shape=jax.ShapeD...]
    ppermute x2 -> x3, starting transfers between devices: 7.95 us -> 5.98 us  [the longest x1 2.22 us: shards(): from_r = lax.ppermute(wide, 'tgt', around[-1])]
    ppermute x3, waiting for transfers between devices: 5.84 us -> 6.94 us  [shards(): lax.ppermute(pair[d].astype(bf16), 'src', xshift[d]).astype(f32)]
    ppermute x3, starting transfers between devices: 4.36 us -> 3.3 us  [shards(): lax.ppermute(pair[d].astype(bf16), 'src', xshift[d]).astype(f32)]
  transfers between devices with their start and end apart: 18 -> 16, of which waited for: 8 -> 8; matrix products, arithmetic and copies ran while one was open for 0% -> 0% of each run, Pallas kernels for 28% -> 26%
where the time goes in v1:
time: 86.3 us; the launch traced here: 86 us
  Pallas kernels  38.6 us (45%)
  starting transfers between devices  26.6 us (31%)
  waiting for transfers between devices  19.5 us (23%)
  other arithmetic  1 us (1%)
    pallas_call x2, Pallas kernels, halo(): pl.pallas_call(functools.partial(halo_kernel, base), out_shape=jax.ShapeD...  9.49 us
    pallas_call x1, Pallas kernels, shards(): pl.pallas_call(node_kernel, out_shape=jax.ShapeDtypeStruct((2, 4, 16, TL_...  8.42 us
    pallas_call x1, Pallas kernels, shards(): pl.pallas_call(top_kernel, out_shape=jax.ShapeDtypeStruct((2, 16, half *...  7.65 us
    pallas_call x1, Pallas kernels, shards(): pl.pallas_call(leaf_kernel, out_shape=(OUT((24, 256, Q), bf16), OUT((24,...  7.52 us
    ppermute x3, waiting for transfers between devices, shards(): lax.ppermute(pair[d].astype(bf16), 'src', xshift[d]).astype(f32)  6.94 us
    ppermute x3, starting transfers between devices, shards(): lax.ppermute(top_pair[d].astype(bf16), 'src', xshift[d]).astype(f32)  5.73 us
    pallas_call x1, Pallas kernels, shards(): pl.pallas_call(own_kernel, out_shape=(jax.ShapeDtypeStruct((WIN + 1, TLEA...  5.49 us
    ppermute x3, starting transfers between devices, others(): return [lax.ppermute(x, axis, shifts[d]) for d in (1, 3, 2)]  5.41 us
  transfers between devices with their start and end apart: 16, of which 8 were waited for; matrix products, arithmetic and copies ran while one was open for 0% of the time, Pallas kernels for 26%

profile of v1, /device:TPU:8, one launch (start us, length us, event | category | flops | bytes accessed | tf_op | source)
XLA Modules:
  0.0 86.0 jit_solution(11055693083584163673)
XLA Ops:
  0.0 7.5 %leaf_stage.1 = (bf16[24,256,128]{2,1,0:T(8,128)(2,1)S(1)}, bf16[24,16,256]{2,1,0:T(8,128)(2,1)S(1)}, bf16[288,128]{1,0:T(8,128)(2,1)S(1)}, bf16[4,96,128]{2,1,0...) custom-call(s32[8,512]{1,0:T(8,128)} %idx_h.1, s32[8,256]{1,0:T(8,128)} %piv_h.1, ...), custom_call_target="tpu_custom_call" | custom-call | flops 8000000000 | bytes 8000000 | tf_op jit(solution)/shard_map/leaf_stage/pallas_call | solution.py:427
  7.5 0.1 collective-permute-start
  7.6 1.3 %collective-permute-done = bf16[4,96,128]{2,1,0:T(8,128)(2,1)S(1)} collective-permute-done((bf16[4,96,128]{2,1,0:T(8,128)(2,1)S(1)}, bf16[4,96,128]{2,1,0:T(8,128)(2,1)S(1)}, u32[]{:S(2)}, u32[]{:S(2)}) %collective-permute-start) | collective-permute-done | bytes 98336 | tf_op jit(solution)/shard_map/ppermute | solution.py:485
  9.0 1.6 %collective-permute-start.1 = (bf16[96,128]{1,0:T(8,128)(2,1)S(1)}, bf16[96,128]{1,0:T(8,128)(2,1)S(1)}, u32[]{:S(2)}, u32[]{:S(2)}) collective-permute-start(bf16[96,128]{1,0:T(8,128)(2,1)S(1)} %get-tuple-element.30), channel_id=1, source_target_pairs={{0,32},{16,48},{32,64},{48,80},{64,96},{80,112},{96,0},{112,16},{1... | collective-permute-start | bytes 73736 | tf_op jit(solution)/shard_map/ppermute | solution.py:488
  10.5 2.7 %collective-permute-start.3 = (bf16[96,128]{1,0:T(8,128)(2,1)S(1)}, bf16[96,128]{1,0:T(8,128)(2,1)S(1)}, u32[]{:S(2)}, u32[]{:S(2)}) collective-permute-start(bf16[96,128]{1,0:T(8,128)(2,1)S(1)} %get-tuple-element.31), channel_id=1, source_target_pairs={{0,64},{16,80},{32,96},{48,112},{64,0},{80,16},{96,32},{112,48},{1... | collective-permute-start | bytes 73736 | tf_op jit(solution)/shard_map/ppermute | solution.py:488
  13.3 1.4 %collective-permute-start.2 = (bf16[96,128]{1,0:T(8,128)(2,1)S(1)}, bf16[96,128]{1,0:T(8,128)(2,1)S(1)}, u32[]{:S(2)}, u32[]{:S(2)}) collective-permute-start(bf16[96,128]{1,0:T(8,128)(2,1)S(1)} %get-tuple-element.32), channel_id=1, source_target_pairs={{0,96},{16,112},{32,0},{48,16},{64,32},{80,48},{96,64},{112,80},{1... | collective-permute-start | bytes 73736 | tf_op jit(solution)/shard_map/ppermute | solution.py:488
  14.7 0.0 collective-permute-done.1
  14.7 1.1 %collective-permute-done.3 = bf16[96,128]{1,0:T(8,128)(2,1)S(1)} collective-permute-done((bf16[96,128]{1,0:T(8,128)(2,1)S(1)}, bf16[96,128]{1,0:T(8,128)(2,1)S(1)}, u32[]{:S(2)}, u32[]{:S(2)}) %collective-permute-start.3) | collective-permute-done | bytes 24608 | tf_op jit(solution)/shard_map/ppermute | solution.py:488
  15.8 1.2 %collective-permute-done.2 = bf16[96,128]{1,0:T(8,128)(2,1)S(1)} collective-permute-done((bf16[96,128]{1,0:T(8,128)(2,1)S(1)}, bf16[96,128]{1,0:T(8,128)(2,1)S(1)}, u32[]{:S(2)}, u32[]{:S(2)}) %collective-permute-start.2) | collective-permute-done | bytes 24608 | tf_op jit(solution)/shard_map/ppermute | solution.py:488
  17.1 2.0 %collective-permute-start.5 = (bf16[704,128]{1,0:T(8,128)(2,1)S(1)}, bf16[704,128]{1,0:T(8,128)(2,1)S(1)}, u32[]{:S(2)}, u32[]{:S(2)}) collective-permute-start(bf16[704,128]{1,0:T(8,128)(2,1)S(1)} %pad_maximum_fusion.after), channel_id=1, source_target_pairs={{0,1},{1,2},{2,3},{3,4},{4,5},{5,6},{6,7},{7,8},{8,9},{9,10},{10,1... | collective-permute-start | bytes 540680 | tf_op jit(solution)/shard_map/ppermute | solution.py:491
  19.1 2.2 %collective-permute-start.4 = (bf16[704,128]{1,0:T(8,128)(2,1)S(1)}, bf16[704,128]{1,0:T(8,128)(2,1)S(1)}, u32[]{:S(2)}, u32[]{:S(2)}) collective-permute-start(bf16[704,128]{1,0:T(8,128)(2,1)S(1)} %pad_maximum_fusion.after), channel_id=1, source_target_pairs={{0,15},{1,0},{2,1},{3,2},{4,3},{5,4},{6,5},{7,6},{8,7},{9,8},{10,9... | collective-permute-start | bytes 540680 | tf_op jit(solution)/shard_map/ppermute | solution.py:492
  21.3 1.8 %collective-permute-start.8 = (bf16[384,128]{1,0:T(8,128)(2,1)S(1)}, bf16[384,128]{1,0:T(8,128)(2,1)S(1)}, u32[]{:S(2)}, u32[]{:S(2)}) collective-permute-start(bf16[384,128]{1,0:T(8,128)(2,1)S(1)} %pad_maximum_fusion.1), channel_id=1, source_target_pairs={{0,2},{1,3},{2,4},{3,5},{4,6},{5,7},{6,8},{7,9},{8,10},{9,11},{10,... | collective-permute-start | bytes 294920 | tf_op jit(solution)/shard_map/ppermute | solution.py:493
  23.1 5.5 %own_terms.1 = (f32[7,256,128]{2,1,0:T(8,128)S(1)}, bf16[17,256,16]{2,1,0:T(8,128)(2,1)S(1)}) custom-call(s32[32,16]{1,0:T(8,128)S(1)} %get-tuple-element.13.lists, bf16[320,128]{1,0:T(8,128)(2,1)S(1)} %get-tuple-element.14.held, bf16[24,256,128]{2,1,0:T(8,128)(2,1)S(1)} %get-tuple-element.15.v_ref, bf16[24,16,256]{2,1,0:T(8,128)(2,1)S(1)} %get-tuple-element.16.f_ref, ...), custom_call_target="tpu_custom_call" | custom-call | flops 5000000000 | bytes 3000000 | tf_op jit(solution)/shard_map/own_terms/pallas_call | solution.py:516
  28.6 0.0 collective-permute-done.5.held
  28.7 0.0 collective-permute-done.8
  28.7 0.0 collective-permute-done.4.held
  28.7 3.9 %collective-permute-start.11 = (bf16[1536,128]{1,0:T(8,128)(2,1)S(1)}, bf16[1536,128]{1,0:T(8,128)(2,1)S(1)}, u32[]{:S(2)}, u32[]{:S(2)}) collective-permute-start(bf16[1536,128]{1,0:T(8,128)(2,1)S(1)} %slice_dynamic-update-slice_fusion.y0), channel_id=1, source_target_pairs={{0,12},{1,13},{2,14},{3,15},{4,0},{5,1},{6,2},{7,3},{8,4},{9,5},{1... | collective-permute-start | bytes 1179656 | tf_op jit(solution)/shard_map/ppermute | solution.py:480
  32.6 0.0 collective-permute-start.10
  32.6 1.6 %collective-permute-start.9 = (bf16[1536,128]{1,0:T(8,128)(2,1)S(1)}, bf16[1536,128]{1,0:T(8,128)(2,1)S(1)}, u32[]{:S(2)}, u32[]{:S(2)}) collective-permute-start(bf16[1536,128]{1,0:T(8,128)(2,1)S(1)} %slice_dynamic-update-slice_fusion.y0), channel_id=1, source_target_pairs={{0,4},{1,5},{2,6},{3,7},{4,8},{5,9},{6,10},{7,11},{8,12},{9,13},{1... | collective-permute-start | bytes 1179656 | tf_op jit(solution)/shard_map/ppermute | solution.py:480
  34.1 4.0 %halo_terms.2.after = bf16[1536,128]{1,0:T(8,128)(2,1)S(1)} custom-call(s32[32,16]{1,0:T(8,128)S(1)} %slice_convert_fusion.lists, bf16[704,128]{1,0:T(8,128)(2,1)S(1)} %collective-permute-done.5.held, bf16[24,256,128]{2,1,0:T(8,128)(2,1)S(1)} %get-tuple-element.15.v_ref, bf16[24,16,256]{2,1,0:T(8,128)(2,1)S(1)} %get-tuple-element.16.f_ref, ...), custom_call_target="tpu_custom_call" | custom-call | flops 1000000000 | bytes 3000000 | tf_op jit(solution)/shard_map/halo_terms/pallas_call | solution.py:500
  38.2 0.0 copy-start
  38.2 0.0 copy-start.1
  38.2 4.1 %collective-permute-start.7 = (bf16[1536,128]{1,0:T(8,128)(2,1)S(1)}, bf16[1536,128]{1,0:T(8,128)(2,1)S(1)}, u32[]{:S(2)}, u32[]{:S(2)}) collective-permute-start(bf16[1536,128]{1,0:T(8,128)(2,1)S(1)} %halo_terms.2.after), channel_id=1, source_target_pairs={{1,0},{2,1},{3,2},{4,3},{5,4},{6,5},{7,6},{8,7},{9,8},{10,9},{11,1... | collective-permute-start | bytes 1179656 | tf_op jit(solution)/shard_map/ppermute | solution.py:535
  42.3 5.5 %halo_terms.3 = bf16[1536,128]{1,0:T(8,128)(2,1)S(1)} custom-call(s32[32,16]{1,0:T(8,128)S(1)} %slice_convert_fusion.1.lists, bf16[704,128]{1,0:T(8,128)(2,1)S(1)} %collective-permute-done.4.held, bf16[24,256,128]{2,1,0:T(8,128)(2,1)S(1)} %get-tuple-element.15.v_ref, bf16[24,16,256]{2,1,0:T(8,128)(2,1)S(1)} %get-tuple-element.16.f_ref, ...), custom_call_target="tpu_custom_call" | custom-call | flops 1000000000 | bytes 3000000 | tf_op jit(solution)/shard_map/halo_terms/pallas_call | solution.py:500
  47.8 1.9 %collective-permute-start.6 = (bf16[1536,128]{1,0:T(8,128)(2,1)S(1)}, bf16[1536,128]{1,0:T(8,128)(2,1)S(1)}, u32[]{:S(2)}, u32[]{:S(2)}) collective-permute-start(bf16[1536,128]{1,0:T(8,128)(2,1)S(1)} %halo_terms.3), channel_id=1, source_target_pairs={{0,1},{1,2},{2,3},{3,4},{4,5},{5,6},{6,7},{7,8},{8,9},{9,10},{10,1... | collective-permute-start | bytes 1179656 | tf_op jit(solution)/shard_map/ppermute | solution.py:537
  49.7 0.0 collective-permute-done.11.y3
  49.7 0.9 %collective-permute-done.10.y2 = bf16[1536,128]{1,0:T(8,128)(2,1)S(1)} collective-permute-done((bf16[1536,128]{1,0:T(8,128)(2,1)S(1)}, bf16[1536,128]{1,0:T(8,128)(2,1)S(1)}, u32[]{:S(2)}, u32[]{:S(2)}) %collective-permute-start.10) | collective-permute-done | bytes 393248 | tf_op jit(solution)/shard_map/ppermute | solution.py:480
  50.6 0.0 collective-permute-done.9.y1
  50.6 0.0 copy-done
  50.6 0.0 copy-done.1
  50.6 7.6 %top_terms.1.top = f32[2,16,2048]{2,1,0:T(8,128)S(1)} custom-call(s32[16,12]{1,0:T(8,128)S(1)} %copy-done, s32[16]{0:T(128)S(1)} %copy-done.1, bf16[17,256,16]{2,1,0:T(8,128)(2,1)S(1)} %get-tuple-element.20.a_all.a_ref, bf16[1536,128]{1,0:T(8,128)(2,1)S(1)} %slice_dynamic-update-slice_fusion.y0, bf16[1536,128]{1,0:T(8,128)(2,1)S(1)} %collective-permute-done.9.y1, ...), custom_call_target="tpu_custom_call" | custom-call | flops 6000000000 | bytes 3000000 | tf_op jit(solution)/shard_map/top_terms/pallas_call | solution.py:540
  58.2 5.4 %collective-permute-done.6.halo_l = bf16[1536,128]{1,0:T(8,128)(2,1)S(1)} collective-permute-done((bf16[1536,128]{1,0:T(8,128)(2,1)S(1)}, bf16[1536,128]{1,0:T(8,128)(2,1)S(1)}, u32[]{:S(2)}, u32[]{:S(2)}) %collective-permute-start.6) | collective-permute-done | bytes 393248 | tf_op jit(solution)/shard_map/ppermute | solution.py:537
  63.6 0.0 collective-permute-done.7.halo_r
  63.6 8.4 %node_terms.1 = f32[2,4,16,4096]{3,2,1,0:T(8,128)S(1)} custom-call(s32[32,16]{1,0:T(8,128)S(1)} %get-tuple-element.13.lists, f32[7,256,128]{2,1,0:T(8,128)S(1)} %get-tuple-element.19.after.own, bf16[17,256,16]{2,1,0:T(8,128)(2,1)S(1)} %get-tuple-element.20.a_all.a_ref, bf16[1536,128]{1,0:T(8,128)(2,1)S(1)} %collective-permute-done.6.halo_l, ...), custom_call_target="tpu_custom_call" | custom-call | flops 6000000000 | bytes 3000000 | tf_op jit(solution)/shard_map/node_terms/pallas_call | solution.py:558
  72.0 0.1 slice_bitcast_fusion
  72.1 0.1 collective-permute-start.12
  72.2 2.6 %collective-permute-done.12 = f32[4,16,4096]{2,1,0:T(8,128)S(1)} collective-permute-done((f32[4,16,4096]{2,1,0:T(8,128)S(1)}, f32[4,16,4096]{2,1,0:T(8,128)S(1)}, u32[]{:S(2)}, u32[]{:S(2)}) %collective-permute-start.12) | collective-permute-done | bytes 1048608 | tf_op jit(solution)/shard_map/ppermute | solution.py:573
  74.8 0.1 fusion.10
  75.0 0.1 collective-permute-start.13
  75.1 1.3 %collective-permute-start.15 = (bf16[16,4096]{1,0:T(8,128)(2,1)S(1)}, bf16[16,4096]{1,0:T(8,128)(2,1)S(1)}, u32[]{:S(2)}, u32[]{:S(2)}) collective-permute-start(bf16[16,4096]{1,0:T(8,128)(2,1)S(1)} %get-tuple-element.26), channel_id=1, source_target_pairs={{0,64},{16,80},{32,96},{48,112},{64,0},{80,16},{96,32},{112,48},{1... | collective-permute-start | bytes 393224 | tf_op jit(solution)/shard_map/ppermute | solution.py:576
  76.5 1.9 %collective-permute-start.14 = (bf16[16,4096]{1,0:T(8,128)(2,1)S(1)}, bf16[16,4096]{1,0:T(8,128)(2,1)S(1)}, u32[]{:S(2)}, u32[]{:S(2)}) collective-permute-start(bf16[16,4096]{1,0:T(8,128)(2,1)S(1)} %get-tuple-element.27), channel_id=1, source_target_pairs={{0,96},{16,112},{32,0},{48,16},{64,32},{80,48},{96,64},{112,80},{1... | collective-permute-start | bytes 393224 | tf_op jit(solution)/shard_map/ppermute | solution.py:576
  78.3 6.3 %collective-permute-done.13 = bf16[16,4096]{1,0:T(8,128)(2,1)S(1)} collective-permute-done((bf16[16,4096]{1,0:T(8,128)(2,1)S(1)}, bf16[16,4096]{1,0:T(8,128)(2,1)S(1)}, u32[]{:S(2)}, u32[]{:S(2)}) %collective-permute-start.13) | collective-permute-done | bytes 131104 | tf_op jit(solution)/shard_map/ppermute | solution.py:576
  84.7 0.0 collective-permute-done.15
  84.7 0.6 collective-permute-done.14
  85.3 0.8 fusion.4
  (12 shorter events, 0.2 us)
Async XLA Ops:
  7.5 1.4 %collective-permute-start = (bf16[4,96,128]{2,1,0:T(8,128)(2,1)S(1)}, bf16[4,96,128]{2,1,0:T(8,128)(2,1)S(1)}, u32[]{:S(2)}, u32[]{:S(2)}) collective-permute-start(bf16[4,96,128]{2,1,0:T(8,128)(2,1)S(1)} %get-tuple-element.18), channel_id=1, source_target_pairs={{0,16},{16,0},{32,48},{48,32},{64,80},{80,64},{96,112},{112,96},{1... | collective-permute-start | bytes 294920 | tf_op jit(solution)/shard_map/ppermute | solution.py:485
  9.0 5.7 %collective-permute-start.1 = (bf16[96,128]{1,0:T(8,128)(2,1)S(1)}, bf16[96,128]{1,0:T(8,128)(2,1)S(1)}, u32[]{:S(2)}, u32[]{:S(2)}) collective-permute-start(bf16[96,128]{1,0:T(8,128)(2,1)S(1)} %get-tuple-element.30), channel_id=1, source_target_pairs={{0,32},{16,48},{32,64},{48,80},{64,96},{80,112},{96,0},{112,16},{1... | collective-permute-start | bytes 73736 | tf_op jit(solution)/shard_map/ppermute | solution.py:488
  10.5 5.3 %collective-permute-start.3 = (bf16[96,128]{1,0:T(8,128)(2,1)S(1)}, bf16[96,128]{1,0:T(8,128)(2,1)S(1)}, u32[]{:S(2)}, u32[]{:S(2)}) collective-permute-start(bf16[96,128]{1,0:T(8,128)(2,1)S(1)} %get-tuple-element.31), channel_id=1, source_target_pairs={{0,64},{16,80},{32,96},{48,112},{64,0},{80,16},{96,32},{112,48},{1... | collective-permute-start | bytes 73736 | tf_op jit(solution)/shard_map/ppermute | solution.py:488
  13.3 3.8 %collective-permute-start.2 = (bf16[96,128]{1,0:T(8,128)(2,1)S(1)}, bf16[96,128]{1,0:T(8,128)(2,1)S(1)}, u32[]{:S(2)}, u32[]{:S(2)}) collective-permute-start(bf16[96,128]{1,0:T(8,128)(2,1)S(1)} %get-tuple-element.32), channel_id=1, source_target_pairs={{0,96},{16,112},{32,0},{48,16},{64,32},{80,48},{96,64},{112,80},{1... | collective-permute-start | bytes 73736 | tf_op jit(solution)/shard_map/ppermute | solution.py:488
  17.1 11.5 %collective-permute-start.5 = (bf16[704,128]{1,0:T(8,128)(2,1)S(1)}, bf16[704,128]{1,0:T(8,128)(2,1)S(1)}, u32[]{:S(2)}, u32[]{:S(2)}) collective-permute-start(bf16[704,128]{1,0:T(8,128)(2,1)S(1)} %pad_maximum_fusion.after), channel_id=1, source_target_pairs={{0,1},{1,2},{2,3},{3,4},{4,5},{5,6},{6,7},{7,8},{8,9},{9,10},{10,1... | collective-permute-start | bytes 540680 | tf_op jit(solution)/shard_map/ppermute | solution.py:491
  19.1 9.6 %collective-permute-start.4 = (bf16[704,128]{1,0:T(8,128)(2,1)S(1)}, bf16[704,128]{1,0:T(8,128)(2,1)S(1)}, u32[]{:S(2)}, u32[]{:S(2)}) collective-permute-start(bf16[704,128]{1,0:T(8,128)(2,1)S(1)} %pad_maximum_fusion.after), channel_id=1, source_target_pairs={{0,15},{1,0},{2,1},{3,2},{4,3},{5,4},{6,5},{7,6},{8,7},{9,8},{10,9... | collective-permute-start | bytes 540680 | tf_op jit(solution)/shard_map/ppermute | solution.py:492
  21.3 7.3 %collective-permute-start.8 = (bf16[384,128]{1,0:T(8,128)(2,1)S(1)}, bf16[384,128]{1,0:T(8,128)(2,1)S(1)}, u32[]{:S(2)}, u32[]{:S(2)}) collective-permute-start(bf16[384,128]{1,0:T(8,128)(2,1)S(1)} %pad_maximum_fusion.1), channel_id=1, source_target_pairs={{0,2},{1,3},{2,4},{3,5},{4,6},{5,7},{6,8},{7,9},{8,10},{9,11},{10,... | collective-permute-start | bytes 294920 | tf_op jit(solution)/shard_map/ppermute | solution.py:493
  28.7 21.0 %collective-permute-start.11 = (bf16[1536,128]{1,0:T(8,128)(2,1)S(1)}, bf16[1536,128]{1,0:T(8,128)(2,1)S(1)}, u32[]{:S(2)}, u32[]{:S(2)}) collective-permute-start(bf16[1536,128]{1,0:T(8,128)(2,1)S(1)} %slice_dynamic-update-slice_fusion.y0), channel_id=1, source_target_pairs={{0,12},{1,13},{2,14},{3,15},{4,0},{5,1},{6,2},{7,3},{8,4},{9,5},{1... | collective-permute-start | bytes 1179656 | tf_op jit(solution)/shard_map/ppermute | solution.py:480
  32.6 18.0 %collective-permute-start.10 = (bf16[1536,128]{1,0:T(8,128)(2,1)S(1)}, bf16[1536,128]{1,0:T(8,128)(2,1)S(1)}, u32[]{:S(2)}, u32[]{:S(2)}) collective-permute-start(bf16[1536,128]{1,0:T(8,128)(2,1)S(1)} %slice_dynamic-update-slice_fusion.y0), channel_id=1, source_target_pairs={{0,8},{1,9},{2,10},{3,11},{4,12},{5,13},{6,14},{7,15},{8,0},{9,1},... | collective-permute-start | bytes 1179656 | tf_op jit(solution)/shard_map/ppermute | solution.py:480
  32.6 18.0 %collective-permute-start.9 = (bf16[1536,128]{1,0:T(8,128)(2,1)S(1)}, bf16[1536,128]{1,0:T(8,128)(2,1)S(1)}, u32[]{:S(2)}, u32[]{:S(2)}) collective-permute-start(bf16[1536,128]{1,0:T(8,128)(2,1)S(1)} %slice_dynamic-update-slice_fusion.y0), channel_id=1, source_target_pairs={{0,4},{1,5},{2,6},{3,7},{4,8},{5,9},{6,10},{7,11},{8,12},{9,13},{1... | collective-permute-start | bytes 1179656 | tf_op jit(solution)/shard_map/ppermute | solution.py:480
  38.2 12.4 %copy-start = (s32[16,12]{1,0:T(8,128)S(1)}, s32[16,12]{1,0:T(8,128)}, u32[]{:S(2)}) copy-start(s32[16,12]{1,0:T(8,128)} %listed.1) | copy-start | bytes 2308
  38.2 12.4 %copy-start.1 = (s32[16]{0:T(128)S(1)}, s32[16]{0:T(128)}, u32[]{:S(2)}) copy-start(s32[16]{0:T(128)} %counts.1) | copy-start | bytes 196
  38.2 25.4 %collective-permute-start.7 = (bf16[1536,128]{1,0:T(8,128)(2,1)S(1)}, bf16[1536,128]{1,0:T(8,128)(2,1)S(1)}, u32[]{:S(2)}, u32[]{:S(2)}) collective-permute-start(bf16[1536,128]{1,0:T(8,128)(2,1)S(1)} %halo_terms.2.after), channel_id=1, source_target_pairs={{1,0},{2,1},{3,2},{4,3},{5,4},{6,5},{7,6},{8,7},{9,8},{10,9},{11,1... | collective-permute-start | bytes 1179656 | tf_op jit(solution)/shard_map/ppermute | solution.py:535
  47.8 15.8 %collective-permute-start.6 = (bf16[1536,128]{1,0:T(8,128)(2,1)S(1)}, bf16[1536,128]{1,0:T(8,128)(2,1)S(1)}, u32[]{:S(2)}, u32[]{:S(2)}) collective-permute-start(bf16[1536,128]{1,0:T(8,128)(2,1)S(1)} %halo_terms.3), channel_id=1, source_target_pairs={{0,1},{1,2},{2,3},{3,4},{4,5},{5,6},{6,7},{7,8},{8,9},{9,10},{10,1... | collective-permute-start | bytes 1179656 | tf_op jit(solution)/shard_map/ppermute | solution.py:537
  72.1 2.7 %collective-permute-start.12 = (f32[4,16,4096]{2,1,0:T(8,128)S(1)}, f32[4,16,4096]{2,1,0:T(8,128)S(1)}, u32[]{:S(2)}, u32[]{:S(2)}) collective-permute-start(f32[4,16,4096]{2,1,0:T(8,128)S(1)} %slice_bitcast_fusion), channel_id=1, source_target_pairs={{0,16},{16,0},{32,48},{48,32},{64,80},{80,64},{96,112},{112,96},{1... | collective-permute-start | bytes 3145736 | tf_op jit(solution)/shard_map/ppermute | solution.py:573
  75.0 9.6 %collective-permute-start.13 = (bf16[16,4096]{1,0:T(8,128)(2,1)S(1)}, bf16[16,4096]{1,0:T(8,128)(2,1)S(1)}, u32[]{:S(2)}, u32[]{:S(2)}) collective-permute-start(bf16[16,4096]{1,0:T(8,128)(2,1)S(1)} %get-tuple-element.25), channel_id=1, source_target_pairs={{0,32},{16,48},{32,64},{48,80},{64,96},{80,112},{96,0},{112,16},{1... | collective-permute-start | bytes 393224 | tf_op jit(solution)/shard_map/ppermute | solution.py:576
  75.1 9.5 %collective-permute-start.15 = (bf16[16,4096]{1,0:T(8,128)(2,1)S(1)}, bf16[16,4096]{1,0:T(8,128)(2,1)S(1)}, u32[]{:S(2)}, u32[]{:S(2)}) collective-permute-start(bf16[16,4096]{1,0:T(8,128)(2,1)S(1)} %get-tuple-element.26), channel_id=1, source_target_pairs={{0,64},{16,80},{32,96},{48,112},{64,0},{80,16},{96,32},{112,48},{1... | collective-permute-start | bytes 393224 | tf_op jit(solution)/shard_map/ppermute | solution.py:576
  76.5 8.8 %collective-permute-start.14 = (bf16[16,4096]{1,0:T(8,128)(2,1)S(1)}, bf16[16,4096]{1,0:T(8,128)(2,1)S(1)}, u32[]{:S(2)}, u32[]{:S(2)}) collective-permute-start(bf16[16,4096]{1,0:T(8,128)(2,1)S(1)} %get-tuple-element.27), channel_id=1, source_target_pairs={{0,96},{16,112},{32,0},{48,16},{64,32},{80,48},{96,64},{112,80},{1... | collective-permute-start | bytes 393224 | tf_op jit(solution)/shard_map/ppermute | solution.py:576

commit v2 on v1

--- a/solution.py
+++ b/solution.py
@@ -180,21 +180,26 @@
 
     lax.fori_loop(0, rows // 512, widen, 0)
 
-    def gather(k, _):
-        at = pl.multiple_of(k * 64, 64)
-        for r in range(64):
-            gathered[pl.ds(at + r, 1), :] = wide[pl.ds(idx_s[at + r], 1), :]
-        return 0
-
-    lax.fori_loop(0, rows // 64, gather, 0)
     for copy in copies[6:9]:
         copy.wait()
 
-    for leaf in range(SL):
-        leaf_vals = gathered[leaf * LEAF : (leaf + 1) * LEAF, :].astype(bf16)
+    def project(leaf):
+        at = pl.multiple_of(leaf * LEAF, LEAF)
+        leaf_vals = gathered[pl.ds(at, LEAF), :].astype(bf16)
         v_out[2 * leaf] = leaf_vals[:256]
         v_out[2 * leaf + 1] = leaf_vals[256:]
         v_out[16 + leaf] = jnp.dot(proj[leaf], leaf_vals, preferred_element_type=f32).astype(bf16)
+
+    def gather(leaf, _):
+        project(jnp.maximum(leaf - 1, 0))
+        at = pl.multiple_of(leaf * LEAF, LEAF)
+        for r in range(LEAF):
+            gathered[pl.ds(at + r, 1), :] = wide[pl.ds(idx_s[at + r], 1), :]
+        return 0
+
+    gathered[0:LEAF, :] = jnp.zeros((LEAF, Q), f32)
+    lax.fori_loop(0, SL, gather, 0)
+    project(SL - 1)
     node_vals = jnp.dot(
         nproj[0], v_out[16:24].reshape(SL * SKEL, Q), preferred_element_type=f32
     ).astype(bf16)

time: 86.3 us -> 86.3 us (level)
  waiting for transfers between devices: 19.5 us -> 17.6 us
  Pallas kernels: 38.6 us -> 39.5 us
    ppermute x1, waiting for transfers between devices: 5.36 us -> 4.09 us  [shards(): got_l = lax.ppermute(to_r, 'tgt', forward)]
    pallas_call x1, Pallas kernels: 7.52 us -> 8.71 us  [shards(): pl.pallas_call(leaf_kernel, out_shape=(OUT((24, 256, Q), bf16), OUT((24,...]
    ppermute x3, starting transfers between devices: 3.3 us -> 4.42 us  [shards(): lax.ppermute(pair[d].astype(bf16), 'src', xshift[d]).astype(f32)]
  transfers between devices with their start and end apart: 16 -> 16, of which waited for: 8 -> 8; matrix products, arithmetic and copies ran while one was open for 0% -> 0% of each run, Pallas kernels for 26% -> 27%
where the time goes in v2:
time: 86.3 us; the launch traced here: 85.8 us
  Pallas kernels  39.5 us (46%)
  starting transfers between devices  27.4 us (32%)
  waiting for transfers between devices  17.6 us (20%)
  other arithmetic  1 us (1%)
    pallas_call x2, Pallas kernels, halo(): pl.pallas_call(functools.partial(halo_kernel, base), out_shape=jax.ShapeD...  10.1 us
    pallas_call x1, Pallas kernels, shards(): pl.pallas_call(leaf_kernel, out_shape=(OUT((24, 256, Q), bf16), OUT((24,...  8.71 us
    pallas_call x1, Pallas kernels, shards(): pl.pallas_call(node_kernel, out_shape=jax.ShapeDtypeStruct((2, 4, 16, TL_...  7.8 us
    pallas_call x1, Pallas kernels, shards(): pl.pallas_call(top_kernel, out_shape=jax.ShapeDtypeStruct((2, 16, half *...  7.65 us
    ppermute x3, waiting for transfers between devices, shards(): lax.ppermute(pair[d].astype(bf16), 'src', xshift[d]).astype(f32)  6.31 us
    ppermute x3, starting transfers between devices, shards(): lax.ppermute(top_pair[d].astype(bf16), 'src', xshift[d]).astype(f32)  5.72 us
    ppermute x3, starting transfers between devices, others(): return [lax.ppermute(x, axis, shifts[d]) for d in (1, 3, 2)]  5.71 us
    pallas_call x1, Pallas kernels, shards(): pl.pallas_call(own_kernel, out_shape=(jax.ShapeDtypeStruct((WIN + 1, TLEA...  5.2 us
  transfers between devices with their start and end apart: 16, of which 8 were waited for; matrix products, arithmetic and copies ran while one was open for 0% of the time, Pallas kernels for 27%

profile of v2, /device:TPU:8, one launch (start us, length us, event | category | flops | bytes accessed | tf_op | source)
XLA Modules:
  0.0 85.8 jit_solution(15219473314598882035)
XLA Ops:
  0.0 8.7 %leaf_stage.1 = (bf16[24,256,128]{2,1,0:T(8,128)(2,1)S(1)}, bf16[24,16,256]{2,1,0:T(8,128)(2,1)S(1)}, bf16[288,128]{1,0:T(8,128)(2,1)S(1)}, bf16[4,96,128]{2,1,0...) custom-call(s32[8,512]{1,0:T(8,128)} %idx_h.1, s32[8,256]{1,0:T(8,128)} %piv_h.1, ...), custom_call_target="tpu_custom_call" | custom-call | flops 8000000000 | bytes 8000000 | tf_op jit(solution)/shard_map/leaf_stage/pallas_call | solution.py:432
  8.7 0.1 collective-permute-start
  8.8 1.3 %collective-permute-done = bf16[4,96,128]{2,1,0:T(8,128)(2,1)S(1)} collective-permute-done((bf16[4,96,128]{2,1,0:T(8,128)(2,1)S(1)}, bf16[4,96,128]{2,1,0:T(8,128)(2,1)S(1)}, u32[]{:S(2)}, u32[]{:S(2)}) %collective-permute-start) | collective-permute-done | bytes 98336 | tf_op jit(solution)/shard_map/ppermute | solution.py:490
  10.1 1.5 %collective-permute-start.1 = (bf16[96,128]{1,0:T(8,128)(2,1)S(1)}, bf16[96,128]{1,0:T(8,128)(2,1)S(1)}, u32[]{:S(2)}, u32[]{:S(2)}) collective-permute-start(bf16[96,128]{1,0:T(8,128)(2,1)S(1)} %get-tuple-element.30), channel_id=1, source_target_pairs={{0,32},{16,48},{32,64},{48,80},{64,96},{80,112},{96,0},{112,16},{1... | collective-permute-start | bytes 73736 | tf_op jit(solution)/shard_map/ppermute | solution.py:493
  11.7 2.7 %collective-permute-start.3 = (bf16[96,128]{1,0:T(8,128)(2,1)S(1)}, bf16[96,128]{1,0:T(8,128)(2,1)S(1)}, u32[]{:S(2)}, u32[]{:S(2)}) collective-permute-start(bf16[96,128]{1,0:T(8,128)(2,1)S(1)} %get-tuple-element.31), channel_id=1, source_target_pairs={{0,64},{16,80},{32,96},{48,112},{64,0},{80,16},{96,32},{112,48},{1... | collective-permute-start | bytes 73736 | tf_op jit(solution)/shard_map/ppermute | solution.py:493
  14.4 1.5 %collective-permute-start.2 = (bf16[96,128]{1,0:T(8,128)(2,1)S(1)}, bf16[96,128]{1,0:T(8,128)(2,1)S(1)}, u32[]{:S(2)}, u32[]{:S(2)}) collective-permute-start(bf16[96,128]{1,0:T(8,128)(2,1)S(1)} %get-tuple-element.32), channel_id=1, source_target_pairs={{0,96},{16,112},{32,0},{48,16},{64,32},{80,48},{96,64},{112,80},{1... | collective-permute-start | bytes 73736 | tf_op jit(solution)/shard_map/ppermute | solution.py:493
  15.9 0.0 collective-permute-done.1
  15.9 1.1 %collective-permute-done.3 = bf16[96,128]{1,0:T(8,128)(2,1)S(1)} collective-permute-done((bf16[96,128]{1,0:T(8,128)(2,1)S(1)}, bf16[96,128]{1,0:T(8,128)(2,1)S(1)}, u32[]{:S(2)}, u32[]{:S(2)}) %collective-permute-start.3) | collective-permute-done | bytes 24608 | tf_op jit(solution)/shard_map/ppermute | solution.py:493
  17.0 1.2 %collective-permute-done.2 = bf16[96,128]{1,0:T(8,128)(2,1)S(1)} collective-permute-done((bf16[96,128]{1,0:T(8,128)(2,1)S(1)}, bf16[96,128]{1,0:T(8,128)(2,1)S(1)}, u32[]{:S(2)}, u32[]{:S(2)}) %collective-permute-start.2) | collective-permute-done | bytes 24608 | tf_op jit(solution)/shard_map/ppermute | solution.py:493
  18.3 2.0 %collective-permute-start.5 = (bf16[704,128]{1,0:T(8,128)(2,1)S(1)}, bf16[704,128]{1,0:T(8,128)(2,1)S(1)}, u32[]{:S(2)}, u32[]{:S(2)}) collective-permute-start(bf16[704,128]{1,0:T(8,128)(2,1)S(1)} %pad_maximum_fusion.after), channel_id=1, source_target_pairs={{0,1},{1,2},{2,3},{3,4},{4,5},{5,6},{6,7},{7,8},{8,9},{9,10},{10,1... | collective-permute-start | bytes 540680 | tf_op jit(solution)/shard_map/ppermute | solution.py:496
  20.3 2.2 %collective-permute-start.4 = (bf16[704,128]{1,0:T(8,128)(2,1)S(1)}, bf16[704,128]{1,0:T(8,128)(2,1)S(1)}, u32[]{:S(2)}, u32[]{:S(2)}) collective-permute-start(bf16[704,128]{1,0:T(8,128)(2,1)S(1)} %pad_maximum_fusion.after), channel_id=1, source_target_pairs={{0,15},{1,0},{2,1},{3,2},{4,3},{5,4},{6,5},{7,6},{8,7},{9,8},{10,9... | collective-permute-start | bytes 540680 | tf_op jit(solution)/shard_map/ppermute | solution.py:497
  22.5 1.8 %collective-permute-start.8 = (bf16[384,128]{1,0:T(8,128)(2,1)S(1)}, bf16[384,128]{1,0:T(8,128)(2,1)S(1)}, u32[]{:S(2)}, u32[]{:S(2)}) collective-permute-start(bf16[384,128]{1,0:T(8,128)(2,1)S(1)} %pad_maximum_fusion.1), channel_id=1, source_target_pairs={{0,2},{1,3},{2,4},{3,5},{4,6},{5,7},{6,8},{7,9},{8,10},{9,11},{10,... | collective-permute-start | bytes 294920 | tf_op jit(solution)/shard_map/ppermute | solution.py:498
  24.3 5.2 %own_terms.1 = (f32[7,256,128]{2,1,0:T(8,128)S(1)}, bf16[17,256,16]{2,1,0:T(8,128)(2,1)S(1)}) custom-call(s32[32,16]{1,0:T(8,128)S(1)} %get-tuple-element.13.lists, bf16[320,128]{1,0:T(8,128)(2,1)S(1)} %get-tuple-element.14.held, bf16[24,256,128]{2,1,0:T(8,128)(2,1)S(1)} %get-tuple-element.15.v_ref, bf16[24,16,256]{2,1,0:T(8,128)(2,1)S(1)} %get-tuple-element.16.f_ref, ...), custom_call_target="tpu_custom_call" | custom-call | flops 5000000000 | bytes 3000000 | tf_op jit(solution)/shard_map/own_terms/pallas_call | solution.py:521
  29.5 0.0 collective-permute-done.5.held
  29.5 0.0 collective-permute-done.8
  29.6 0.0 collective-permute-done.4.held
  29.6 4.2 %collective-permute-start.11 = (bf16[1536,128]{1,0:T(8,128)(2,1)S(1)}, bf16[1536,128]{1,0:T(8,128)(2,1)S(1)}, u32[]{:S(2)}, u32[]{:S(2)}) collective-permute-start(bf16[1536,128]{1,0:T(8,128)(2,1)S(1)} %slice_dynamic-update-slice_fusion.y0), channel_id=1, source_target_pairs={{0,12},{1,13},{2,14},{3,15},{4,0},{5,1},{6,2},{7,3},{8,4},{9,5},{1... | collective-permute-start | bytes 1179656 | tf_op jit(solution)/shard_map/ppermute | solution.py:485
  33.8 0.0 collective-permute-start.10
  33.8 1.6 %collective-permute-start.9 = (bf16[1536,128]{1,0:T(8,128)(2,1)S(1)}, bf16[1536,128]{1,0:T(8,128)(2,1)S(1)}, u32[]{:S(2)}, u32[]{:S(2)}) collective-permute-start(bf16[1536,128]{1,0:T(8,128)(2,1)S(1)} %slice_dynamic-update-slice_fusion.y0), channel_id=1, source_target_pairs={{0,4},{1,5},{2,6},{3,7},{4,8},{5,9},{6,10},{7,11},{8,12},{9,13},{1... | collective-permute-start | bytes 1179656 | tf_op jit(solution)/shard_map/ppermute | solution.py:485
  35.3 4.7 %halo_terms.2.after = bf16[1536,128]{1,0:T(8,128)(2,1)S(1)} custom-call(s32[32,16]{1,0:T(8,128)S(1)} %slice_convert_fusion.lists, bf16[704,128]{1,0:T(8,128)(2,1)S(1)} %collective-permute-done.5.held, bf16[24,256,128]{2,1,0:T(8,128)(2,1)S(1)} %get-tuple-element.15.v_ref, bf16[24,16,256]{2,1,0:T(8,128)(2,1)S(1)} %get-tuple-element.16.f_ref, ...), custom_call_target="tpu_custom_call" | custom-call | flops 1000000000 | bytes 3000000 | tf_op jit(solution)/shard_map/halo_terms/pallas_call | solution.py:505
  40.0 0.0 copy-start
  40.0 0.0 copy-start.1
  40.0 3.4 %collective-permute-start.7 = (bf16[1536,128]{1,0:T(8,128)(2,1)S(1)}, bf16[1536,128]{1,0:T(8,128)(2,1)S(1)}, u32[]{:S(2)}, u32[]{:S(2)}) collective-permute-start(bf16[1536,128]{1,0:T(8,128)(2,1)S(1)} %halo_terms.2.after), channel_id=1, source_target_pairs={{1,0},{2,1},{3,2},{4,3},{5,4},{6,5},{7,6},{8,7},{9,8},{10,9},{11,1... | collective-permute-start | bytes 1179656 | tf_op jit(solution)/shard_map/ppermute | solution.py:540
  43.5 5.5 %halo_terms.3 = bf16[1536,128]{1,0:T(8,128)(2,1)S(1)} custom-call(s32[32,16]{1,0:T(8,128)S(1)} %slice_convert_fusion.1.lists, bf16[704,128]{1,0:T(8,128)(2,1)S(1)} %collective-permute-done.4.held, bf16[24,256,128]{2,1,0:T(8,128)(2,1)S(1)} %get-tuple-element.15.v_ref, bf16[24,16,256]{2,1,0:T(8,128)(2,1)S(1)} %get-tuple-element.16.f_ref, ...), custom_call_target="tpu_custom_call" | custom-call | flops 1000000000 | bytes 3000000 | tf_op jit(solution)/shard_map/halo_terms/pallas_call | solution.py:505
  49.0 1.9 %collective-permute-start.6 = (bf16[1536,128]{1,0:T(8,128)(2,1)S(1)}, bf16[1536,128]{1,0:T(8,128)(2,1)S(1)}, u32[]{:S(2)}, u32[]{:S(2)}) collective-permute-start(bf16[1536,128]{1,0:T(8,128)(2,1)S(1)} %halo_terms.3), channel_id=1, source_target_pairs={{0,1},{1,2},{2,3},{3,4},{4,5},{5,6},{6,7},{7,8},{8,9},{9,10},{10,1... | collective-permute-start | bytes 1179656 | tf_op jit(solution)/shard_map/ppermute | solution.py:542
  50.9 0.0 collective-permute-done.11.y3
  50.9 0.9 %collective-permute-done.10.y2 = bf16[1536,128]{1,0:T(8,128)(2,1)S(1)} collective-permute-done((bf16[1536,128]{1,0:T(8,128)(2,1)S(1)}, bf16[1536,128]{1,0:T(8,128)(2,1)S(1)}, u32[]{:S(2)}, u32[]{:S(2)}) %collective-permute-start.10) | collective-permute-done | bytes 393248 | tf_op jit(solution)/shard_map/ppermute | solution.py:485
  51.8 0.0 collective-permute-done.9.y1
  51.8 0.0 copy-done
  51.8 0.0 copy-done.1
  51.8 7.6 %top_terms.1.top = f32[2,16,2048]{2,1,0:T(8,128)S(1)} custom-call(s32[16,12]{1,0:T(8,128)S(1)} %copy-done, s32[16]{0:T(128)S(1)} %copy-done.1, bf16[17,256,16]{2,1,0:T(8,128)(2,1)S(1)} %get-tuple-element.20.a_all.a_ref, bf16[1536,128]{1,0:T(8,128)(2,1)S(1)} %slice_dynamic-update-slice_fusion.y0, bf16[1536,128]{1,0:T(8,128)(2,1)S(1)} %collective-permute-done.9.y1, ...), custom_call_target="tpu_custom_call" | custom-call | flops 6000000000 | bytes 3000000 | tf_op jit(solution)/shard_map/top_terms/pallas_call | solution.py:545
  59.4 4.1 %collective-permute-done.6.halo_l = bf16[1536,128]{1,0:T(8,128)(2,1)S(1)} collective-permute-done((bf16[1536,128]{1,0:T(8,128)(2,1)S(1)}, bf16[1536,128]{1,0:T(8,128)(2,1)S(1)}, u32[]{:S(2)}, u32[]{:S(2)}) %collective-permute-start.6) | collective-permute-done | bytes 393248 | tf_op jit(solution)/shard_map/ppermute | solution.py:542
  63.5 0.0 collective-permute-done.7.halo_r
  63.5 7.8 %node_terms.1 = f32[2,4,16,4096]{3,2,1,0:T(8,128)S(1)} custom-call(s32[32,16]{1,0:T(8,128)S(1)} %get-tuple-element.13.lists, f32[7,256,128]{2,1,0:T(8,128)S(1)} %get-tuple-element.19.after.own, bf16[17,256,16]{2,1,0:T(8,128)(2,1)S(1)} %get-tuple-element.20.a_all.a_ref, bf16[1536,128]{1,0:T(8,128)(2,1)S(1)} %collective-permute-done.6.halo_l, ...), custom_call_target="tpu_custom_call" | custom-call | flops 6000000000 | bytes 3000000 | tf_op jit(solution)/shard_map/node_terms/pallas_call | solution.py:563
  71.3 0.1 slice_bitcast_fusion
  71.4 0.1 collective-permute-start.12
  71.5 2.6 %collective-permute-done.12 = f32[4,16,4096]{2,1,0:T(8,128)S(1)} collective-permute-done((f32[4,16,4096]{2,1,0:T(8,128)S(1)}, f32[4,16,4096]{2,1,0:T(8,128)S(1)}, u32[]{:S(2)}, u32[]{:S(2)}) %collective-permute-start.12) | collective-permute-done | bytes 1048608 | tf_op jit(solution)/shard_map/ppermute | solution.py:578
  74.1 0.1 fusion.10
  74.3 0.1 collective-permute-start.13
  74.4 4.3 %collective-permute-start.15 = (bf16[16,4096]{1,0:T(8,128)(2,1)S(1)}, bf16[16,4096]{1,0:T(8,128)(2,1)S(1)}, u32[]{:S(2)}, u32[]{:S(2)}) collective-permute-start(bf16[16,4096]{1,0:T(8,128)(2,1)S(1)} %get-tuple-element.26), channel_id=1, source_target_pairs={{0,64},{16,80},{32,96},{48,112},{64,0},{80,16},{96,32},{112,48},{1... | collective-permute-start | bytes 393224 | tf_op jit(solution)/shard_map/ppermute | solution.py:581
  78.7 0.0 collective-permute-start.14
  78.8 2.4 %collective-permute-done.13 = bf16[16,4096]{1,0:T(8,128)(2,1)S(1)} collective-permute-done((bf16[16,4096]{1,0:T(8,128)(2,1)S(1)}, bf16[16,4096]{1,0:T(8,128)(2,1)S(1)}, u32[]{:S(2)}, u32[]{:S(2)}) %collective-permute-start.13) | collective-permute-done | bytes 131104 | tf_op jit(solution)/shard_map/ppermute | solution.py:581
  81.1 3.9 %collective-permute-done.15 = bf16[16,4096]{1,0:T(8,128)(2,1)S(1)} collective-permute-done((bf16[16,4096]{1,0:T(8,128)(2,1)S(1)}, bf16[16,4096]{1,0:T(8,128)(2,1)S(1)}, u32[]{:S(2)}, u32[]{:S(2)}) %collective-permute-start.15) | collective-permute-done | bytes 131104 | tf_op jit(solution)/shard_map/ppermute | solution.py:581
  85.1 0.0 collective-permute-done.14
  85.1 0.8 fusion.4
  (12 shorter events, 0.2 us)
Async XLA Ops:
  8.7 1.4 %collective-permute-start = (bf16[4,96,128]{2,1,0:T(8,128)(2,1)S(1)}, bf16[4,96,128]{2,1,0:T(8,128)(2,1)S(1)}, u32[]{:S(2)}, u32[]{:S(2)}) collective-permute-start(bf16[4,96,128]{2,1,0:T(8,128)(2,1)S(1)} %get-tuple-element.18), channel_id=1, source_target_pairs={{0,16},{16,0},{32,48},{48,32},{64,80},{80,64},{96,112},{112,96},{1... | collective-permute-start | bytes 294920 | tf_op jit(solution)/shard_map/ppermute | solution.py:490
  10.1 5.7 %collective-permute-start.1 = (bf16[96,128]{1,0:T(8,128)(2,1)S(1)}, bf16[96,128]{1,0:T(8,128)(2,1)S(1)}, u32[]{:S(2)}, u32[]{:S(2)}) collective-permute-start(bf16[96,128]{1,0:T(8,128)(2,1)S(1)} %get-tuple-element.30), channel_id=1, source_target_pairs={{0,32},{16,48},{32,64},{48,80},{64,96},{80,112},{96,0},{112,16},{1... | collective-permute-start | bytes 73736 | tf_op jit(solution)/shard_map/ppermute | solution.py:493
  11.7 5.3 %collective-permute-start.3 = (bf16[96,128]{1,0:T(8,128)(2,1)S(1)}, bf16[96,128]{1,0:T(8,128)(2,1)S(1)}, u32[]{:S(2)}, u32[]{:S(2)}) collective-permute-start(bf16[96,128]{1,0:T(8,128)(2,1)S(1)} %get-tuple-element.31), channel_id=1, source_target_pairs={{0,64},{16,80},{32,96},{48,112},{64,0},{80,16},{96,32},{112,48},{1... | collective-permute-start | bytes 73736 | tf_op jit(solution)/shard_map/ppermute | solution.py:493
  14.4 3.8 %collective-permute-start.2 = (bf16[96,128]{1,0:T(8,128)(2,1)S(1)}, bf16[96,128]{1,0:T(8,128)(2,1)S(1)}, u32[]{:S(2)}, u32[]{:S(2)}) collective-permute-start(bf16[96,128]{1,0:T(8,128)(2,1)S(1)} %get-tuple-element.32), channel_id=1, source_target_pairs={{0,96},{16,112},{32,0},{48,16},{64,32},{80,48},{96,64},{112,80},{1... | collective-permute-start | bytes 73736 | tf_op jit(solution)/shard_map/ppermute | solution.py:493
  18.3 11.2 %collective-permute-start.5 = (bf16[704,128]{1,0:T(8,128)(2,1)S(1)}, bf16[704,128]{1,0:T(8,128)(2,1)S(1)}, u32[]{:S(2)}, u32[]{:S(2)}) collective-permute-start(bf16[704,128]{1,0:T(8,128)(2,1)S(1)} %pad_maximum_fusion.after), channel_id=1, source_target_pairs={{0,1},{1,2},{2,3},{3,4},{4,5},{5,6},{6,7},{7,8},{8,9},{9,10},{10,1... | collective-permute-start | bytes 540680 | tf_op jit(solution)/shard_map/ppermute | solution.py:496
  20.3 9.3 %collective-permute-start.4 = (bf16[704,128]{1,0:T(8,128)(2,1)S(1)}, bf16[704,128]{1,0:T(8,128)(2,1)S(1)}, u32[]{:S(2)}, u32[]{:S(2)}) collective-permute-start(bf16[704,128]{1,0:T(8,128)(2,1)S(1)} %pad_maximum_fusion.after), channel_id=1, source_target_pairs={{0,15},{1,0},{2,1},{3,2},{4,3},{5,4},{6,5},{7,6},{8,7},{9,8},{10,9... | collective-permute-start | bytes 540680 | tf_op jit(solution)/shard_map/ppermute | solution.py:497
  22.5 7.0 %collective-permute-start.8 = (bf16[384,128]{1,0:T(8,128)(2,1)S(1)}, bf16[384,128]{1,0:T(8,128)(2,1)S(1)}, u32[]{:S(2)}, u32[]{:S(2)}) collective-permute-start(bf16[384,128]{1,0:T(8,128)(2,1)S(1)} %pad_maximum_fusion.1), channel_id=1, source_target_pairs={{0,2},{1,3},{2,4},{3,5},{4,6},{5,7},{6,8},{7,9},{8,10},{9,11},{10,... | collective-permute-start | bytes 294920 | tf_op jit(solution)/shard_map/ppermute | solution.py:498
  29.6 21.3 %collective-permute-start.11 = (bf16[1536,128]{1,0:T(8,128)(2,1)S(1)}, bf16[1536,128]{1,0:T(8,128)(2,1)S(1)}, u32[]{:S(2)}, u32[]{:S(2)}) collective-permute-start(bf16[1536,128]{1,0:T(8,128)(2,1)S(1)} %slice_dynamic-update-slice_fusion.y0), channel_id=1, source_target_pairs={{0,12},{1,13},{2,14},{3,15},{4,0},{5,1},{6,2},{7,3},{8,4},{9,5},{1... | collective-permute-start | bytes 1179656 | tf_op jit(solution)/shard_map/ppermute | solution.py:485
  33.8 18.0 %collective-permute-start.10 = (bf16[1536,128]{1,0:T(8,128)(2,1)S(1)}, bf16[1536,128]{1,0:T(8,128)(2,1)S(1)}, u32[]{:S(2)}, u32[]{:S(2)}) collective-permute-start(bf16[1536,128]{1,0:T(8,128)(2,1)S(1)} %slice_dynamic-update-slice_fusion.y0), channel_id=1, source_target_pairs={{0,8},{1,9},{2,10},{3,11},{4,12},{5,13},{6,14},{7,15},{8,0},{9,1},... | collective-permute-start | bytes 1179656 | tf_op jit(solution)/shard_map/ppermute | solution.py:485
  33.8 18.0 %collective-permute-start.9 = (bf16[1536,128]{1,0:T(8,128)(2,1)S(1)}, bf16[1536,128]{1,0:T(8,128)(2,1)S(1)}, u32[]{:S(2)}, u32[]{:S(2)}) collective-permute-start(bf16[1536,128]{1,0:T(8,128)(2,1)S(1)} %slice_dynamic-update-slice_fusion.y0), channel_id=1, source_target_pairs={{0,4},{1,5},{2,6},{3,7},{4,8},{5,9},{6,10},{7,11},{8,12},{9,13},{1... | collective-permute-start | bytes 1179656 | tf_op jit(solution)/shard_map/ppermute | solution.py:485
  40.0 11.8 %copy-start = (s32[16,12]{1,0:T(8,128)S(1)}, s32[16,12]{1,0:T(8,128)}, u32[]{:S(2)}) copy-start(s32[16,12]{1,0:T(8,128)} %listed.1) | copy-start | bytes 2308
  40.0 11.8 %copy-start.1 = (s32[16]{0:T(128)S(1)}, s32[16]{0:T(128)}, u32[]{:S(2)}) copy-start(s32[16]{0:T(128)} %counts.1) | copy-start | bytes 196
  40.0 23.5 %collective-permute-start.7 = (bf16[1536,128]{1,0:T(8,128)(2,1)S(1)}, bf16[1536,128]{1,0:T(8,128)(2,1)S(1)}, u32[]{:S(2)}, u32[]{:S(2)}) collective-permute-start(bf16[1536,128]{1,0:T(8,128)(2,1)S(1)} %halo_terms.2.after), channel_id=1, source_target_pairs={{1,0},{2,1},{3,2},{4,3},{5,4},{6,5},{7,6},{8,7},{9,8},{10,9},{11,1... | collective-permute-start | bytes 1179656 | tf_op jit(solution)/shard_map/ppermute | solution.py:540
  49.0 14.6 %collective-permute-start.6 = (bf16[1536,128]{1,0:T(8,128)(2,1)S(1)}, bf16[1536,128]{1,0:T(8,128)(2,1)S(1)}, u32[]{:S(2)}, u32[]{:S(2)}) collective-permute-start(bf16[1536,128]{1,0:T(8,128)(2,1)S(1)} %halo_terms.3), channel_id=1, source_target_pairs={{0,1},{1,2},{2,3},{3,4},{4,5},{5,6},{6,7},{7,8},{8,9},{9,10},{10,1... | collective-permute-start | bytes 1179656 | tf_op jit(solution)/shard_map/ppermute | solution.py:542
  71.4 2.7 %collective-permute-start.12 = (f32[4,16,4096]{2,1,0:T(8,128)S(1)}, f32[4,16,4096]{2,1,0:T(8,128)S(1)}, u32[]{:S(2)}, u32[]{:S(2)}) collective-permute-start(f32[4,16,4096]{2,1,0:T(8,128)S(1)} %slice_bitcast_fusion), channel_id=1, source_target_pairs={{0,16},{16,0},{32,48},{48,32},{64,80},{80,64},{96,112},{112,96},{1... | collective-permute-start | bytes 3145736 | tf_op jit(solution)/shard_map/ppermute | solution.py:578
  74.3 6.8 %collective-permute-start.13 = (bf16[16,4096]{1,0:T(8,128)(2,1)S(1)}, bf16[16,4096]{1,0:T(8,128)(2,1)S(1)}, u32[]{:S(2)}, u32[]{:S(2)}) collective-permute-start(bf16[16,4096]{1,0:T(8,128)(2,1)S(1)} %get-tuple-element.25), channel_id=1, source_target_pairs={{0,32},{16,48},{32,64},{48,80},{64,96},{80,112},{96,0},{112,16},{1... | collective-permute-start | bytes 393224 | tf_op jit(solution)/shard_map/ppermute | solution.py:581
  74.4 10.7 %collective-permute-start.15 = (bf16[16,4096]{1,0:T(8,128)(2,1)S(1)}, bf16[16,4096]{1,0:T(8,128)(2,1)S(1)}, u32[]{:S(2)}, u32[]{:S(2)}) collective-permute-start(bf16[16,4096]{1,0:T(8,128)(2,1)S(1)} %get-tuple-element.26), channel_id=1, source_target_pairs={{0,64},{16,80},{32,96},{48,112},{64,0},{80,16},{96,32},{112,48},{1... | collective-permute-start | bytes 393224 | tf_op jit(solution)/shard_map/ppermute | solution.py:581
  78.7 6.3 %collective-permute-start.14 = (bf16[16,4096]{1,0:T(8,128)(2,1)S(1)}, bf16[16,4096]{1,0:T(8,128)(2,1)S(1)}, u32[]{:S(2)}, u32[]{:S(2)}) collective-permute-start(bf16[16,4096]{1,0:T(8,128)(2,1)S(1)} %get-tuple-element.27), channel_id=1, source_target_pairs={{0,96},{16,112},{32,0},{48,16},{64,32},{80,48},{96,64},{112,80},{1... | collective-permute-start | bytes 393224 | tf_op jit(solution)/shard_map/ppermute | solution.py:581
